TPU v7x, 128 devices: a whole 4x4x4 slice. The times are simulated.
128 devices in a mesh: wide: 16 (over x_hi, z, core), node: 8 (over x_lo, y).
Axes of the slice: x: 4 (x_hi: 2, x_lo: 2; x = x_hi * 2 + x_lo), y: 4, z: 4, core: 2. Of those that a mesh axis runs over, the one named last changes fastest.
Arguments:
- tokens: bfloat16 [12288, 3072], P('wide', 'node'), may hold values from -6 to 6
- target: bfloat16 [12288, 3072], P('wide', 'node'), may hold values from -6 to 6
- mod_table: bfloat16 [32, 3072], P(None, 'node'), may hold values from -1.5 to 1.5
- adv_table: float32 [32, 16], replicated, may hold values from 0.25 to 4
- w_up: bfloat16 [3072, 7168], P('wide', 'node'), may hold values from -0.109375 to 0.109375
- w_down_t: bfloat16 [3072, 7168], P('wide', 'node'), may hold values from -0.0625 to 0.0625
- bins: int32 [48], P('wide'), may hold values from 0 to 31
- groups: int32 [48], P('wide'), may hold values from 0 to 15
Outputs:
- grad_tokens: float32 [12288, 3072], P('wide', 'node')
- grad_up: float32 [3072, 7168], P('wide', 'node')
- grad_down: float32 [3072, 7168], P('wide', 'node')
All inputs are finite; a program needn't handle non-finite values.
Results may differ from a plain program's by a relative error of at most 0.02.
Values may be sent and summed in bfloat16 or wider, within the bound.
A program may use at most 128 MiB of HBM per device.

v0:
```python
import jax
import jax.numpy as jnp
from jax import lax
from jax.sharding import PartitionSpec as P


def gelu_tanh(value):
    return jax.nn.gelu(value, approximate=True)


def contract_last(left, right):
    return lax.dot_general(
        left, right, (((1,), (1,)), ((), ())), preferred_element_type=jnp.float32
    )


def on_device(tokens, target, mod_table, adv_table, w_up, w_down_t, bins, groups):
    full_tok, full_mod = (
        lax.all_gather(tokens, "node", axis=1, tiled=True),
        lax.all_gather(mod_table, "node", axis=1, tiled=True),
    )
    rows = tokens.shape[0]
    micro = bins.shape[0]
    seq = rows // micro
    width = full_tok.shape[1]
    local_width = tokens.shape[1]
    bin_hot = (bins[:, None] == jnp.arange(adv_table.shape[0])[None, :]).astype(jnp.float32)
    grp_hot = (groups[:, None] == jnp.arange(adv_table.shape[1])[None, :]).astype(jnp.float32)
    high = lax.Precision.HIGHEST
    gain_full = 1.0 + jnp.dot(bin_hot, full_mod.astype(jnp.float32), precision=high)
    gain_local = 1.0 + jnp.dot(bin_hot, mod_table.astype(jnp.float32), precision=high)
    weight = jnp.sum(jnp.dot(bin_hot, adv_table, precision=high) * grp_hot, axis=1)
    modulated = (
        (full_tok.reshape(micro, seq, width).astype(jnp.float32) * gain_full[:, None, :])
        .astype(jnp.bfloat16)
        .reshape(rows, width)
    )
    hidden_cols = w_up.shape[1]

    def fold_rows(left, piece):
        return jnp.dot(left, piece, preferred_element_type=jnp.float32)

    def map_rows(left, piece):
        return contract_last(left, piece)

    pre = fold_rows(modulated, lax.all_gather(w_up, "wide", axis=0, tiled=True))
    hidden = gelu_tanh(pre).astype(jnp.bfloat16)
    delta_part = map_rows(hidden, lax.all_gather(w_down_t, "wide", axis=0, tiled=True))
    delta = lax.psum_scatter(
        delta_part.astype(jnp.bfloat16), "node", scatter_dimension=1, tiled=True
    ).astype(jnp.float32)
    err = tokens.astype(jnp.float32) + delta - target.astype(jnp.float32)
    dpred = (err.reshape(micro, seq, local_width) * weight[:, None, None]).reshape(
        rows, local_width
    )
    dy = dpred.astype(jnp.bfloat16)
    dy_full = lax.all_gather(dy, "node", axis=1, tiled=True)
    pull = jax.vjp(gelu_tanh, pre)[1]
    dh = fold_rows(dy_full, lax.all_gather(w_down_t, "wide", axis=0, tiled=True))
    dpre = pull(dh)[0].astype(jnp.bfloat16)
    dmod_part = map_rows(dpre, lax.all_gather(w_up, "wide", axis=0, tiled=True))
    dmod = lax.psum_scatter(
        dmod_part.astype(jnp.bfloat16), "node", scatter_dimension=1, tiled=True
    ).astype(jnp.float32)
    grad_tokens = dpred + (gain_local[:, None, :] * dmod.reshape(micro, seq, local_width)).reshape(
        rows, local_width
    )
    scale = float(lax.axis_size("wide") * rows) ** (-0.5)
    term_up = lax.dot_general(
        modulated, dpre, (((0,), (0,)), ((), ())), preferred_element_type=jnp.float32
    )
    term_down = lax.dot_general(
        dy_full, hidden, (((0,), (0,)), ((), ())), preferred_element_type=jnp.float32
    )
    summed = lax.psum_scatter(
        (jnp.concatenate([term_up, term_down], axis=1) * scale).astype(jnp.bfloat16),
        "wide",
        scatter_dimension=0,
        tiled=True,
    ).astype(jnp.float32)
    grad_up = summed[:, :hidden_cols]
    grad_down = summed[:, hidden_cols:]
    return (grad_tokens, grad_up, grad_down)


def solution(mesh):
    return jax.shard_map(
        on_device,
        mesh=mesh,
        in_specs=(
            P("wide", "node"),
            P("wide", "node"),
            P(None, "node"),
            P(),
            P("wide", "node"),
            P("wide", "node"),
            P("wide"),
            P("wide"),
        ),
        out_specs=(P("wide", "node"), P("wide", "node"), P("wide", "node")),
        check_vma=False,
    )
```

profile of v0, /device:TPU:2, one launch (start us, length us, event | category | flops | bytes accessed | tf_op | source)
XLA Modules:
  0.0 536.8 jit_solution(9273582299312235300)
XLA Ops:
  9.4 29.0 %all_gather.18 = bf16[32,3072]{1,0:T(8,128)(2,1)S(1)} all-gather(bf16[32,384]{1,0:T(8,128)(2,1)} %param.10), channel_id=1, replica_groups=mesh['wide'=16,'node'=8] {'node'}, dimensions={1}, use_global_device_ids=true | all-gather | bytes 221184 | tf_op jit(solution)/shard_map/all_gather | solution.py:20
  39.3 30.8 %all-gather.5.cloned.1.call-done = bf16[768,3072]{1,0:T(8,128)(2,1)} async-done(((bf16[768,384]{1,0:T(8,128)(2,1)}), bf16[768,3072]{1,0:T(8,128)(2,1)}) %all-gather.5.cloned.1.call-update) | async-done | bytes 4718608 | tf_op jit(solution)/shard_map/all_gather | solution.py:19
  70.1 5.7 %fusion.1 = bf16[768,3072]{1,0:T(8,128)(2,1)} fusion(bf16[768,3072]{1,0:T(8,128)(2,1)} %all-gather.5.cloned.1.call-done, f32[3,3072]{1,0:T(4,128)S(1)} %convolution_add_fusion), kind=kLoop, calls=%fused_computation.3 | loop fusion | flops 7077888 | bytes 9474048 | tf_op jit(solution)/shard_map/convert_element_type | solution.py:35
  75.8 56.4 %all-gather.7.cloned.1.call-done = bf16[3072,896]{1,0:T(8,128)(2,1)} async-done(((bf16[192,896]{1,0:T(8,128)(2,1)}), bf16[3072,896]{1,0:T(8,128)(2,1)}) %all-gather.7.cloned.1.call-update) | async-done | bytes 5505040 | tf_op jit(solution)/shard_map/all_gather | solution.py:46
  132.2 8.5 %fusion.17 = f32[768,896]{1,0:T(8,128)S(1)} fusion(bf16[768,3072]{1,0:T(8,128)(2,1)} %fusion.1, bf16[3072,896]{1,0:T(8,128)(2,1)} %all-gather.7.cloned.1.call-done), kind=kOutput, calls=%fused_computation.31 | convolution fusion | flops 4227858432 | bytes 12976128 | tf_op jit(solution)/shard_map/dot_general | solution.py:41
  140.7 52.7 %all-gather.9.cloned.1.call-done = bf16[3072,896]{1,0:T(8,128)(2,1)} async-done(((bf16[192,896]{1,0:T(8,128)(2,1)}), bf16[3072,896]{1,0:T(8,128)(2,1)}) %all-gather.9.cloned.1.call-update) | async-done | bytes 5505040 | tf_op jit(solution)/shard_map/all_gather | solution.py:48
  193.4 9.4 %convolution_convert_fusion.1 = bf16[768,3072]{1,0:T(8,128)(2,1)} fusion(bf16[3072,896]{1,0:T(8,128)(2,1)} %all-gather.9.cloned.1.call-done, f32[768,896]{1,0:T(8,128)S(1)} %fusion.17), kind=kOutput, calls=%fused_computation.5 | convolution fusion | flops 4236410880 | bytes 12976128 | tf_op jit(solution)/shard_map/dot_general | solution.py:12
  202.8 6.6 %copy.15 = bf16[768,3072]{0,1:T(8,128)(2,1)} copy(bf16[768,3072]{1,0:T(8,128)(2,1)} %convolution_convert_fusion.1) | data formatting | bytes 9437184
  210.5 54.9 %reduce-scatter.10.cloned.1.call-done = bf16[384,768]{1,0:T(8,128)(2,1)} async-done(((bf16[3072,768]{1,0:T(8,128)(2,1)}), bf16[384,768]{1,0:T(8,128)(2,1)}) %reduce-scatter.10.cloned.1.call-update) | async-done | bytes 589840
  265.4 1.4 copy.16
  267.9 56.4 %all-gather.11.cloned.1.call-done = bf16[768,3072]{1,0:T(8,128)(2,1)} async-done(((bf16[768,384]{1,0:T(8,128)(2,1)}), bf16[768,3072]{1,0:T(8,128)(2,1)}) %all-gather.11.cloned.1.call-update) | async-done | bytes 4718608 | tf_op jit(solution)/shard_map/all_gather | solution.py:57
  324.4 10.0 %fusion.8 = bf16[768,896]{1,0:T(8,128)(2,1)S(1)} fusion(f32[768,896]{1,0:T(8,128)} %copy-done.7, bf16[768,3072]{1,0:T(8,128)(2,1)} %all-gather.11.cloned.1.call-done, bf16[3072,896]{1,0:T(8,128)(2,1)} %all-gather.9.cloned.1.call-done), kind=kOutput, calls=%fused_computation.15 | convolution fusion | flops 4241620992 | bytes 14352384 | tf_op jit(solution)/shard_map/dot_general | solution.py:41
  335.4 9.3 %convolution_convert_fusion = bf16[768,3072]{1,0:T(8,128)(2,1)} fusion(bf16[768,896]{1,0:T(8,128)(2,1)S(1)} %fusion.8, bf16[3072,896]{1,0:T(8,128)(2,1)} %all-gather.7.cloned.1.call-done), kind=kOutput, calls=%fused_computation.4 | convolution fusion | flops 4230217728 | bytes 11599872 | tf_op jit(solution)/shard_map/dot_general | solution.py:12
  344.7 6.6 %copy.17 = bf16[768,3072]{0,1:T(8,128)(2,1)} copy(bf16[768,3072]{1,0:T(8,128)(2,1)} %convolution_convert_fusion) | data formatting | bytes 9437184
  351.6 6.9 %fusion.18 = f32[3072,896]{0,1:T(8,128)S(1)} fusion(bf16[768,3072]{1,0:T(8,128)(2,1)} %fusion.1, bf16[768,896]{1,0:T(8,128)(2,1)} %copy-done.9), kind=kOutput, calls=%fused_computation.32 | convolution fusion | flops 4227858432 | bytes 17104896 | tf_op jit(solution)/shard_map/dot_general | solution.py:69
  358.6 6.9 %fusion.15 = f32[3072,896]{0,1:T(8,128)S(1)} fusion(bf16[768,3072]{1,0:T(8,128)(2,1)} %all-gather.11.cloned.1.call-done, f32[768,896]{1,0:T(8,128)S(1)} %copy-done.8), kind=kOutput, calls=%fused_computation.29 | convolution fusion | flops 4234051584 | bytes 18481152 | tf_op jit(solution)/shard_map/dot_general | solution.py:72
  365.5 6.3 %fusion = bf16[3072,1792]{0,1:T(8,128)(2,1)} fusion(f32[3072,896]{0,1:T(8,128)S(1)} %fusion.15, f32[3072,896]{0,1:T(8,128)S(1)} %fusion.18), kind=kLoop, calls=%fused_computation.1 | loop fusion | flops 16515072 | bytes 33030144 | tf_op jit(solution)/shard_map/convert_element_type | solution.py:76
  371.8 14.3 %copy.19 = bf16[3072,1792]{1,0:T(8,128)(2,1)} copy(bf16[3072,1792]{0,1:T(8,128)(2,1)} %fusion) | data formatting | bytes 22020096
  387.1 21.3 %reduce-scatter.12.cloned.1.call-done = bf16[384,768]{1,0:T(8,128)(2,1)} async-done(((bf16[3072,768]{1,0:T(8,128)(2,1)}), bf16[384,768]{1,0:T(8,128)(2,1)}) %reduce-scatter.12.cloned.1.call-update) | async-done | bytes 589840
  408.3 1.4 copy.18
  409.7 1.4 fusion.9
  411.1 115.0 %reduce-scatter.14.cloned.1.call-done = bf16[192,1792]{1,0:T(8,128)(2,1)} async-done(((bf16[3072,1792]{1,0:T(8,128)(2,1)}), bf16[192,1792]{1,0:T(8,128)(2,1)}) %reduce-scatter.14.cloned.1.call-update) | async-done | bytes 688144
  526.1 1.4 copy.20
  527.7 1.1 copy.14
  (42 shorter events, 8.7 us)
Async XLA Ops:
  7.2 202.4 %copy-start = (f32[32,16]{0,1:T(8,128)S(1)}, f32[32,16]{0,1:T(8,128)}, u32[]{:S(2)}) copy-start(f32[32,16]{0,1:T(8,128)} %param.11) | copy-start | bytes 6148
  7.2 62.9 %all-gather.5.cloned.1.call-start = ((), (), s32[]{:S(2)}) async-start(), calls=%async_computation.3 | async-start | bytes 5308416 | tf_op jit(solution)/shard_map/all_gather | solution.py:19
  7.9 124.3 %all-gather.7.cloned.1.call-start = ((), (), s32[]{:S(2)}) async-start(), calls=%async_computation.4 | async-start | bytes 5849088 | tf_op jit(solution)/shard_map/all_gather | solution.py:46
  8.7 184.7 %all-gather.9.cloned.1.call-start = ((), (), s32[]{:S(2)}) async-start(), calls=%async_computation.5 | async-start | bytes 5849088 | tf_op jit(solution)/shard_map/all_gather | solution.py:48
  9.4 256.0 %reduce-scatter.10.cloned.1.call-start = ((), (), s32[]{:S(2)}) async-start(), calls=%async_computation.7 | async-start | bytes 5308416
  140.7 62.1 %copy-start.7 = (f32[768,896]{1,0:T(8,128)}, f32[768,896]{1,0:T(8,128)S(1)}, u32[]{:S(2)}) copy-start(f32[768,896]{1,0:T(8,128)S(1)} %fusion.17) | copy-start | bytes 8257540
  209.4 0.7 copy-start.5
  209.4 0.7 copy-start.6
  209.4 57.3 %copy-start.2 = (bf16[768,384]{1,0:T(8,128)(2,1)S(1)}, bf16[768,384]{1,0:T(8,128)(2,1)}, u32[]{:S(2)}) copy-start(bf16[768,384]{1,0:T(8,128)(2,1)} %param.8) | copy-start | bytes 1769476
  209.4 57.4 %copy-start.3 = (bf16[768,384]{1,0:T(8,128)(2,1)S(1)}, bf16[768,384]{1,0:T(8,128)(2,1)}, u32[]{:S(2)}) copy-start(bf16[768,384]{1,0:T(8,128)(2,1)} %param.9) | copy-start | bytes 1769476
  209.5 114.9 %all-gather.11.cloned.1.call-start = ((), (), s32[]{:S(2)}) async-start(), calls=%async_computation.6 | async-start | bytes 5308416 | tf_op jit(solution)/shard_map/all_gather | solution.py:57
  267.9 140.4 %reduce-scatter.12.cloned.1.call-start = ((), (), s32[]{:S(2)}) async-start(), calls=%async_computation.8 | async-start | bytes 5308416
  334.4 1.1 copy-start.9
  351.4 174.7 %reduce-scatter.14.cloned.1.call-start = ((), (), s32[]{:S(2)}) async-start(), calls=%async_computation.9 | async-start | bytes 11698176
  351.6 7.0 %copy-start.8 = (f32[768,896]{1,0:T(8,128)S(1)}, f32[768,896]{1,0:T(8,128)}, u32[]{:S(2)}) copy-start(f32[768,896]{1,0:T(8,128)} %copy-done.7) | copy-start | bytes 8257540
  386.1 0.7 copy-start.4
  526.1 3.9 copy-start.1
Sparse Core Ops, SparseCore 0:
  9.7 60.3 all-gather.4
  72.5 59.5 all-gather.6
  134.7 58.7 all-gather.8
  209.6 55.7 reduce-scatter.9
  268.0 56.3 all-gather.10
  351.5 56.7 reduce-scatter.11
  412.7 113.3 reduce-scatter.13
where the time goes:
time: 539 us; the launch traced here: 537 us
  waiting for transfers between devices  390 us (72%)
  matrix products  52.4 us (10%)
  local copies, waits for them, and re-layouts  36.6 us (7%)
  blocking collectives  29 us (5%)
  other arithmetic  14.5 us (3%)
  between operations  14.3 us (3%)
    unnamed x10, waiting for transfers between devices  193 us
    all_gather x1, waiting for transfers between devices, on_device(): dy_full = lax.all_gather(dy, 'node', axis=1, tiled=True)  56.4 us
    all_gather x1, waiting for transfers between devices, on_device(): pre = fold_rows(modulated, lax.all_gather(w_up, 'wide', axis=0, tiled=True))  56.4 us
    all_gather x1, waiting for transfers between devices, on_device(): lax.all_gather(w_down_t, 'wide', axis=0, tiled=True)  52.7 us
    unnamed x28, local copies, waits for them, and re-layouts  36.3 us
    all_gather x1, waiting for transfers between devices, on_device(): lax.all_gather(tokens, 'node', axis=1, tiled=True)  30.8 us
    all_gather x1, blocking collectives, on_device(): lax.all_gather(mod_table, 'node', axis=1, tiled=True)  29 us
    dot_general x2, matrix products, contract_last(): lax.dot_general(left, right, (((1,), (1,)), ((), ())), preferred_element_...  18.7 us
  transfers between devices with their start and end apart: 7, of which 7 were waited for; matrix products, arithmetic and copies ran while one was open for 10% of the time, Pallas kernels for 0%

commit v1 on v0

v1 whole, which is shorter than its diff:
```python
import jax
import jax.numpy as jnp
from jax import lax
from jax.experimental import pallas as pl
from jax.experimental.pallas import tpu as pltpu
from jax.sharding import PartitionSpec as P

F32 = jnp.float32
BF16 = jnp.bfloat16
MESH = pl.DeviceIdType.MESH
COEF = 0.7978845608028654


def dot_nn(a, b):
    return jnp.dot(a, b, preferred_element_type=F32)


def dot_nt(a, b):
    return lax.dot_general(a, b, (((1,), (1,)), ((), ())), preferred_element_type=F32)


def dot_tn(a, b):
    return lax.dot_general(a, b, (((0,), (0,)), ((), ())), preferred_element_type=F32)


def gelu_slope(v):
    th = jnp.tanh(COEF * (v + 0.044715 * v * v * v))
    return 0.5 * (1.0 + th) + 0.5 * v * (1.0 - th * th) * COEF * (1.0 + 3 * 0.044715 * v * v)


def tiles(rows, size, body):
    @pl.loop(0, rows // size)
    def _(t):
        body(pl.ds(pl.multiple_of(t * size, size), size))


def make_kernel(rows, feat, depth, hidden, micro, scale):
    seq = rows // micro

    def kernel(
        tok, tgt, mod, adv, bins, grps, wu_in, wd_in,
        gt_out, gu_out, gd_out,
        X, Y, Wu, Wd, pre, dh, hid, dpre, SB, RB1, RB2, SGD, SIBD, SIBU, RGD, RGU, gain,
        ss, rs, ls,
    ):
        SGU = Wd
        wi, ni = lax.axis_index("wide"), lax.axis_index("node")
        xh, z, c = wi // 8, (wi // 2) % 4, wi % 2
        xl, y = ni // 4, ni % 4

        def nd(dx, dy):
            return ((xl + dx) % 2) * 4 + (y + dy + 4) % 4

        def wm(dx, dz):
            return ((xh + dx) % 2) * 4 + (z + dz + 4) % 4

        def dnode(dx, dy):
            return (wi, nd(dx, dy))

        def dwide(dx, dz):
            return (wm(dx, dz) * 2 + c, ni)

        sib = (wm(0, 0) * 2 + 1 - c, ni)

        table = {}
        count = [0]

        def add(name, src, dst, got, dev):
            table[name] = (count[0], src, dst, got, dev)
            count[0] += 1

        def desc(name, received):
            i, src, dst, got, dev = table[name]
            return pltpu.make_async_remote_copy(
                src_ref=got if received else src,
                dst_ref=got if received else dst,
                send_sem=ss.at[i],
                recv_sem=rs.at[i],
                device_id=dev,
                device_id_type=MESH,
            )

        def start(*names):
            for name in names:
                desc(name, False).start()

        def recv(*names):
            for name in names:
                desc(name, True).wait_recv()

        def sent(*names):
            for name in names:
                desc(name, False).wait_send()

        half = rows // 2
        H1, H2 = pl.ds(0, half), pl.ds(half, half)

        def add_ag(p, B):
            def one(name, blk, r, got, dev):
                add(p + name, B.at[blk, r], B.at[blk, r], B.at[got, r], dev)

            R = pl.ds(0, rows)
            one("x", nd(0, 0), R, nd(1, 0), dnode(1, 0))
            one("yp", nd(0, 0), R, nd(0, -1), dnode(0, 1))
            one("ym", nd(0, 0), R, nd(0, 1), dnode(0, -1))
            one("cp", nd(0, -1), H1, nd(0, 2), dnode(0, 1))
            one("cm", nd(0, 1), H2, nd(0, 2), dnode(0, -1))
            one("bp", nd(1, 0), R, nd(1, -1), dnode(0, 1))
            one("bm", nd(1, 0), R, nd(1, 1), dnode(0, -1))
            one("d1", nd(0, 2), H1, nd(1, 2), dnode(1, 0))
            one("d2", nd(0, 2), H2, nd(1, 2), dnode(1, 0))

        AGN = ("x", "yp", "ym", "cp", "cm", "bp", "bm", "d1", "d2")
        part = depth // 16
        mine, other = pl.multiple_of(c * part, part), pl.multiple_of((1 - c) * part, part)
        PC, PS = pl.ds(mine, part), pl.ds(other, part)
        Q1 = pl.ds(mine, part // 2)
        Q2 = pl.ds(pl.multiple_of(mine + part // 2, part // 2), part // 2)
        SIBS = ((0, 0), (0, -1), (0, 1), (1, 0), (0, 2), (1, -1), (1, 1), (1, 2))

        def add_wag(p, B):
            def one(name, blk, r, got, dev):
                add(p + name, B.at[blk, r], B.at[blk, r], B.at[got, r], dev)

            one("x", wm(0, 0), PC, wm(1, 0), dwide(1, 0))
            one("zp", wm(0, 0), PC, wm(0, -1), dwide(0, 1))
            one("zm", wm(0, 0), PC, wm(0, 1), dwide(0, -1))
            one("cp", wm(0, -1), Q1, wm(0, 2), dwide(0, 1))
            one("cm", wm(0, 1), Q2, wm(0, 2), dwide(0, -1))
            one("bp", wm(1, 0), PC, wm(1, -1), dwide(0, 1))
            one("bm", wm(1, 0), PC, wm(1, 1), dwide(0, -1))
            one("ep", wm(1, -1), Q1, wm(1, 2), dwide(0, 1))
            one("em", wm(1, 1), Q2, wm(1, 2), dwide(0, -1))
            for dx, dz in SIBS:
                b = wm(dx, dz)
                add(f"{p}s{dx}{dz}", B.at[b, PC], B.at[b, PC], B.at[b, PS], sib)

        WAG = ("x", "zp", "zm", "cp", "cm", "bp", "bm", "ep", "em") + tuple(f"s{a}{b}" for a, b in SIBS)

        def add_rs(p, R):
            def one(name, blk, r, slot, dev):
                add(p + name, SB.at[blk, r], R.at[slot, r], R.at[slot, r], dev)

            W = pl.ds(0, rows)
            one("x0", nd(1, 2), W, 0, dnode(1, 0))
            one("bp", nd(1, 1), W, 2, dnode(0, 1))
            one("bm", nd(1, -1), W, 3, dnode(0, -1))
            one("cp", nd(0, 2), H1, 1, dnode(0, 1))
            one("cm", nd(0, 2), H2, 1, dnode(0, -1))
            one("ax", nd(1, 0), W, 4, dnode(1, 0))
            one("ap", nd(0, 1), W, 5, dnode(0, 1))
            one("am", nd(0, -1), W, 6, dnode(0, -1))

        RSN = ("x0", "bp", "bm", "cp", "cm", "ax", "ap", "am")
        A1, A2 = pl.ds(0, part // 2), pl.ds(part // 2, part // 2)
        AW = pl.ds(0, part)

        def add_wrs(p, S, R, B):
            def one(name, blk, r, slot, rr, dev):
                add(p + name, S.at[blk, r], R.at[slot, rr], R.at[slot, rr], dev)

            one("cp0", wm(0, 2), Q1, 0, A1, dwide(0, 1))
            one("cm0", wm(0, 2), Q2, 0, A2, dwide(0, -1))
            one("cp1", wm(1, 2), Q1, 1, A1, dwide(0, 1))
            one("cm1", wm(1, 2), Q2, 1, A2, dwide(0, -1))
            one("bp", wm(1, 1), PC, 2, AW, dwide(0, 1))
            one("bm", wm(1, -1), PC, 3, AW, dwide(0, -1))
            one("ap", wm(0, 1), PC, 4, AW, dwide(0, 1))
            one("am", wm(0, -1), PC, 5, AW, dwide(0, -1))
            one("ax", wm(1, 0), PC, 6, AW, dwide(1, 0))
            base = count[0]
            count[0] += 8

            def sibling(b):
                return pltpu.make_async_remote_copy(
                    src_ref=S.at[b, PS],
                    dst_ref=B.at[b],
                    send_sem=ss.at[base + b],
                    recv_sem=rs.at[base + b],
                    device_id=sib,
                    device_id_type=MESH,
                )

            return sibling

        RSW = ("cp0", "cm0", "cp1", "cm1", "bp", "bm", "ap", "am", "ax")
        add_ag("X", X)
        add_ag("Y", Y)
        add_wag("U", Wu)
        add_wag("D", Wd)
        add_rs("P", RB1)
        add_rs("M", RB2)
        sib_d = add_wrs("G", SGD, RGD, SIBD)
        sib_u = add_wrs("H", SGU, RGU, SIBU)

        barrier = pltpu.get_barrier_semaphore()
        for dev in (dnode(1, 0), dnode(0, 1), dnode(0, -1), dwide(1, 0), dwide(0, 1), dwide(0, -1), sib):
            pl.semaphore_signal(barrier, inc=1, device_id=dev, device_id_type=MESH)
        lu = pltpu.make_async_copy(wu_in, Wu.at[wm(0, 0), PC], ls.at[0])
        ld = pltpu.make_async_copy(wd_in, Wd.at[wm(0, 0), PC], ls.at[1])
        lu.start()
        ld.start()
        nb, ng = adv.shape
        row_i = lax.broadcasted_iota(jnp.int32, (nb, feat), 0)
        for s in range(micro):
            picked = jnp.sum(jnp.where(row_i == bins[s], mod[...].astype(F32), 0.0), axis=0, keepdims=True)
            gain[s : s + 1, :] = 1.0 + picked

            def modulate(r, s=s):
                q = pl.ds(pl.multiple_of(r.start + s * seq, 32), r.size)
                X[nd(0, 0), q, :] = (tok[q, :].astype(F32) * gain[s : s + 1, :]).astype(BF16)

            tiles(seq, 32, modulate)
        lu.wait()
        ld.wait()
        pl.semaphore_wait(barrier, 7)

        start("Xyp", "Xym", "Xx", "Ux", "Uzp", "Uzm", "Us00")

        def zero(r):
            pre[r, :] = jnp.zeros((r.size, hidden), F32)
            dh[r, :] = jnp.zeros((r.size, hidden), F32)

        tiles(rows, 32, zero)
        recv("Uzp")
        start("Ucp", "Us0-1")
        recv("Uzm")
        start("Ucm", "Us01")
        recv("Ux")
        start("Ubp", "Ubm", "Us10")
        start("Dx", "Dzp", "Dzm", "Ds00")
        recv("Xyp")
        start("Xcp")
        recv("Xym")
        start("Xcm")
        recv("Xx")
        start("Xbp", "Xbm")
        recv("Ucp", "Ucm")
        start("Us02")
        recv("Ubp")
        start("Uep", "Us1-1")
        recv("Ubm")
        start("Uem", "Us11")
        recv("Xcp")
        start("Xd1")
        recv("Xcm")
        start("Xd2")
        recv("Dzp")
        start("Dcp", "Ds0-1")
        recv("Dzm")
        start("Dcm", "Ds01")
        recv("Dx")
        start("Dbp", "Dbm", "Ds10")
        recv("Uep", "Uem")
        start("Us12")
        recv(*[f"Us{a}{b}" for a, b in SIBS])

        def arrival(k):
            dx = jnp.where((k == 3) | (k >= 5), 1, 0)
            dy = jnp.where((k == 1) | (k == 5), 1, jnp.where((k == 2) | (k == 6), 3, jnp.where((k == 4) | (k == 7), 2, 0)))
            return ((xl + dx) % 2) * 4 + (y + dy) % 4

        @pl.loop(0, 8)
        def _(k):
            @pl.when(k == 5)
            def _():
                recv("Dcp", "Dcm")
                start("Ds02")
                recv("Dbp")
                start("Dep", "Ds1-1")
                recv("Dbm")
                start("Dem", "Ds11")
                recv("Xbp", "Xbm", "Xd1", "Xd2")

            n = arrival(k)
            pre[...] += dot_nn(X[n], Wu[n])

        def activate(r):
            hid[r, :] = jax.nn.gelu(pre[r, :], approximate=True).astype(BF16)

        tiles(rows, 32, activate)
        recv("Dep", "Dem")
        start("Ds12")
        recv(*[f"Ds{a}{b}" for a, b in SIBS])

        def departure(k):
            dx = jnp.where((k <= 2) | (k == 4), 1, 0)
            dy = jnp.where((k == 0) | (k == 3), 2, jnp.where((k == 1) | (k == 5), 1, jnp.where((k == 2) | (k == 6), 3, 0)))
            return ((xl + dx) % 2) * 4 + (y + dy) % 4

        def products(p, left, weight):
            @pl.loop(0, 8)
            def _(k):
                n = departure(k)
                SB[n] = dot_nt(left[...], weight[n]).astype(BF16)

                @pl.when(k == 0)
                def _():
                    start(p + "x0")

                @pl.when(k == 1)
                def _():
                    start(p + "bp")

                @pl.when(k == 2)
                def _():
                    start(p + "bm")

        def plus(blk, r0, size, R, *slots):
            def body(r):
                q = pl.ds(pl.multiple_of(r.start + r0, 32), r.size)
                v = SB[blk, q, :].astype(F32)
                for slot in slots:
                    v = v + R[slot, q, :].astype(F32)
                SB[blk, q, :] = v.astype(BF16)

            tiles(size, 32, body)

        def rs_first(p, R):
            recv(p + "x0")
            plus(nd(0, 2), 0, rows, R, 0)
            start(p + "cp", p + "cm")

        def rs_second(p, R):
            recv(p + "bp", p + "bm")
            plus(nd(1, 0), 0, rows, R, 2, 3)
            start(p + "ax")

        def rs_third(p, R):
            recv(p + "cp")
            plus(nd(0, 1), 0, half, R, 1)
            start(p + "ap")
            recv(p + "cm")
            plus(nd(0, -1), half, half, R, 1)
            start(p + "am")

        products("P", hid, Wd)
        rs_first("P", RB1)
        rs_second("P", RB1)
        rs_third("P", RB1)
        recv("Pax", "Pap", "Pam")

        def total(R, q):
            v = SB[nd(0, 0), q, :].astype(F32) + R[4, q, :].astype(F32)
            return v + R[5, q, :].astype(F32) + R[6, q, :].astype(F32)

        bin_i = lax.broadcasted_iota(jnp.int32, (nb, ng), 0)
        grp_i = lax.broadcasted_iota(jnp.int32, (nb, ng), 1)
        for s in range(micro):
            chosen = jnp.where((bin_i == bins[s]) & (grp_i == grps[s]), adv[...], 0.0)
            weight = jnp.sum(jnp.sum(chosen, axis=1, keepdims=True), axis=0, keepdims=True)

            def error(r, s=s, weight=weight):
                q = pl.ds(pl.multiple_of(r.start + s * seq, 32), r.size)
                d = weight * (tok[q, :].astype(F32) + total(RB1, q) - tgt[q, :].astype(F32))
                gt_out[q, :] = d
                Y[nd(0, 0), q, :] = d.astype(BF16)

            tiles(seq, 32, error)

        start("Yyp", "Yym", "Yx")
        sent(*["P" + n for n in RSN])

        @pl.loop(0, 8)
        def _(k):
            @pl.when(k == 1)
            def _():
                recv("Yyp")
                start("Ycp")
                recv("Yym")
                start("Ycm")
                recv("Yx")
                start("Ybp", "Ybm")

            @pl.when(k == 4)
            def _():
                recv("Ycp")
                start("Yd1")
                recv("Ycm")
                start("Yd2")

            @pl.when(k == 5)
            def _():
                recv("Ybp", "Ybm", "Yd1", "Yd2")

            n = arrival(k)
            SGD[n] = (dot_tn(Y[n], hid[...]) * scale).astype(BF16)
            sib_d(n).start()
            dh[...] += dot_nn(Y[n], Wd[n])

        def wide_plus(S, blk, slots, r0, size):
            def body(r):
                a = pl.ds(pl.multiple_of(r.start + r0, 32), r.size)
                q = pl.ds(pl.multiple_of(mine + r.start + r0, 32), r.size)
                v = S[blk, q, :].astype(F32)
                for ref, slot in slots:
                    v = v + ref[slot, a, :].astype(F32)
                S[blk, q, :] = v.astype(BF16)

            tiles(size, 32, body)

        def wide_first(p, S, B, sibling):
            for d in ((0, 2), (1, 2)):
                b = wm(*d)
                sibling(b).wait_recv()
                wide_plus(S, b, ((B, b),), 0, part)
            start(p + "cp0", p + "cm0", p + "cp1", p + "cm1")

        def wide_rest(p, S, B, sibling):
            for d in ((1, 1), (1, -1), (0, 1), (0, -1), (1, 0), (0, 0)):
                sibling(wm(*d)).wait_recv()

        quarter = part // 2

        def wide_second(p, S, B, R):
            for dx, cc, kind in ((1, "1", "b"), (0, "0", "a")):
                recv(p + "cp" + cc)
                b = wm(dx, 1)
                wide_plus(S, b, ((B, b), (R, dx)), 0, quarter)
                wide_plus(S, b, ((B, b),), quarter, quarter)
                start(p + kind + "p")
                recv(p + "cm" + cc)
                b = wm(dx, -1)
                wide_plus(S, b, ((B, b),), 0, quarter)
                wide_plus(S, b, ((B, b), (R, dx)), quarter, quarter)
                start(p + kind + "m")

        def wide_third(p, S, B, R):
            recv(p + "bp", p + "bm")
            b = wm(1, 0)
            wide_plus(S, b, ((B, b), (R, 2), (R, 3)), 0, part)
            start(p + "ax")

        def wide_last(p, S, B, R, out):
            recv(p + "ap", p + "am", p + "ax")
            b = wm(0, 0)

            def body(r):
                q = pl.ds(pl.multiple_of(mine + r.start, 32), r.size)
                v = S[b, q, :].astype(F32) + B[b, r, :].astype(F32)
                for slot in (4, 5, 6):
                    v = v + R[slot, r, :].astype(F32)
                out[r, :] = v

            tiles(part, 32, body)

        wide_first("G", SGD, SIBD, sib_d)

        def slope(r):
            dpre[r, :] = (dh[r, :] * gelu_slope(pre[r, :])).astype(BF16)

        tiles(rows, 32, slope)

        products("M", dpre, Wu)
        wide_rest("G", SGD, SIBD, sib_d)
        wide_second("G", SGD, SIBD, RGD)
        sent(*["D" + n for n in WAG])

        def outward(k):
            dx = jnp.where((k == 1) | (k == 2) | (k == 3) | (k == 6), 1, 0)
            dz = jnp.where(k <= 1, 2, jnp.where((k == 2) | (k == 4), 1, jnp.where((k == 3) | (k == 5), 3, 0)))
            return ((xh + dx) % 2) * 4 + (z + dz) % 4

        @pl.loop(0, 8)
        def _(k):
            m = outward(k)
            SGU[m] = (dot_tn(X[m], dpre[...]) * scale).astype(BF16)
            sib_u(m).start()

            @pl.when(k == 3)
            def _():
                wide_first("H", SGU, SIBU, sib_u)

        rs_first("M", RB2)
        wide_third("G", SGD, SIBD, RGD)
        rs_second("M", RB2)
        rs_third("M", RB2)
        wide_rest("H", SGU, SIBU, sib_u)
        wide_second("H", SGU, SIBU, RGU)
        wide_last("G", SGD, SIBD, RGD, gd_out)
        recv("Max", "Map", "Mam")
        for s in range(micro):

            def finish(r, s=s):
                q = pl.ds(pl.multiple_of(r.start + s * seq, 32), r.size)
                gt_out[q, :] = gt_out[q, :] + gain[s : s + 1, :] * total(RB2, q)

            tiles(seq, 32, finish)
        wide_third("H", SGU, SIBU, RGU)
        wide_last("H", SGU, SIBU, RGU, gu_out)

        sent(*["X" + n for n in AGN], *["Y" + n for n in AGN], *["U" + n for n in WAG], *["M" + n for n in RSN])
        sent(*["G" + n for n in RSW], *["H" + n for n in RSW])

        @pl.loop(0, 8)
        def _(b):
            sib_d(b).wait_send()
            sib_u(b).wait_send()

    return kernel


TRANSFERS = 9 * 2 + 17 * 2 + 8 * 2 + 17 * 2


def on_device(tokens, target, mod_table, adv_table, w_up, w_down_t, bins, groups):
    rows, feat = tokens.shape
    part, hidden = w_up.shape
    depth = part * 16
    micro = bins.shape[0]
    scale = float(16 * rows) ** (-0.5)
    vmem = pl.BlockSpec(memory_space=pltpu.VMEM)
    smem = pl.BlockSpec(memory_space=pltpu.SMEM)
    anys = pl.BlockSpec(memory_space=pl.ANY)
    block = (8, rows, feat)
    wblock = (8, depth // 8, hidden)
    V = pltpu.VMEM
    flops = 6 * 2 * rows * depth * hidden
    return pl.pallas_call(
        make_kernel(rows, feat, depth, hidden, micro, scale),
        out_shape=(
            jax.ShapeDtypeStruct((rows, feat), F32),
            jax.ShapeDtypeStruct((part, hidden), F32),
            jax.ShapeDtypeStruct((part, hidden), F32),
        ),
        in_specs=[vmem, vmem, vmem, vmem, smem, smem, anys, anys],
        out_specs=(vmem, vmem, vmem),
        scratch_shapes=[
            V(block, BF16), V(block, BF16), V(wblock, BF16), V(wblock, BF16),
            V((rows, hidden), F32), V((rows, hidden), F32), V((rows, hidden), BF16), V((rows, hidden), BF16),
            V(block, BF16), V((7, rows, feat), BF16), V((7, rows, feat), BF16),
            V(wblock, BF16), V((8, part, hidden), BF16), V((8, part, hidden), BF16),
            V((7, part, hidden), BF16), V((7, part, hidden), BF16),
            V((8, feat), F32),
            pltpu.SemaphoreType.DMA((TRANSFERS,)),
            pltpu.SemaphoreType.DMA((TRANSFERS,)),
            pltpu.SemaphoreType.DMA((2,)),
        ],
        compiler_params=pltpu.CompilerParams(
            collective_id=0, has_side_effects=True, vmem_limit_bytes=63 * 2**20
        ),
        cost_estimate=pl.CostEstimate(flops=flops, bytes_accessed=8 * 2**20, transcendentals=2 * rows * hidden),
        name="block_gradient",
    )(tokens, target, mod_table, adv_table, bins, groups, w_up, w_down_t)


def solution(mesh):
    return jax.shard_map(
        on_device,
        mesh=mesh,
        in_specs=(
            P("wide", "node"),
            P("wide", "node"),
            P(None, "node"),
            P(),
            P("wide", "node"),
            P("wide", "node"),
            P("wide"),
            P("wide"),
        ),
        out_specs=(P("wide", "node"), P("wide", "node"), P("wide", "node")),
        check_vma=False,
    )
```

time: 539 us -> 212 us (0.39)
  waiting for transfers between devices: 390 us -> 0 us
  Pallas kernels: 0 us -> 203 us
  matrix products: 52.4 us -> 0 us
  local copies, waits for them, and re-layouts: 36.6 us -> 6 us
  blocking collectives: 29 us -> 0 us
  other arithmetic: 14.5 us -> 0 us
  between operations: 14.3 us -> 0.65 us
    pallas_call x0 -> x1, Pallas kernels: none -> 203 us  [on_device(): pl.pallas_call(make_kernel(rows, feat, depth, hidden, micro, scale), out_...]
    all_gather x4 -> x0, waiting for transfers between devices: 196 us -> none  [the longest x1 56.4 us: on_device(): dy_full = lax.all_gather(dy, 'node', axis=1, tiled=True)]
    unnamed x10 -> x0, waiting for transfers between devices: 193 us -> none
    dot_general x9 -> x0, matrix products: 52.4 us -> none  [the longest x2 18.7 us: contract_last(): lax.dot_general(left, right, (((1,), (1,)), ((), ())), preferred_element_...]
    unnamed x28 -> x8, local copies, waits for them, and re-layouts: 36.3 us -> 6 us
    all_gather x1 -> x0, blocking collectives: 29 us -> none  [on_device(): lax.all_gather(mod_table, 'node', axis=1, tiled=True)]
    convert_element_type x3 -> x0, other arithmetic: 13.2 us -> none  [the longest x1 6.34 us: on_device(): (jnp.concatenate([term_up, term_down], axis=1) * scale).astype(jnp.bfloat16)]
  transfers between devices with their start and end apart: 7 -> 0, of which waited for: 7 -> 0; matrix products, arithmetic and copies ran while one was open for 10% -> 0% of each run, Pallas kernels for 0% -> 0%
where the time goes in v1:
time: 212 us; the launch traced here: 210 us
  Pallas kernels  203 us (96%)
  local copies, waits for them, and re-layouts  6 us (3%)
    pallas_call x1, Pallas kernels, on_device(): pl.pallas_call(make_kernel(rows, feat, depth, hidden, micro, scale), out_...  203 us
    unnamed x8, local copies, waits for them, and re-layouts  6 us

profile of v1, /device:TPU:2, one launch (start us, length us, event | category | flops | bytes accessed | tf_op | source)
XLA Modules:
  0.0 209.8 jit_solution(18359495522799179172)
XLA Ops:
  0.6 1.4 copy.11.adv
  2.0 203.1 %block_gradient.1 = (f32[768,384]{1,0:T(8,128)}, f32[192,896]{1,0:T(8,128)}, f32[192,896]{1,0:T(8,128)}) custom-call(bf16[768,384]{1,0:T(8,128)(2,1)} %tok.1, bf16[768,384]{1,0:T(8,128)(2,1)} %tgt.1, bf16[32,384]{1,0:T(8,128)(2,1)} %mod.1, f32[32,16]{1,0:T(8,128)} %copy.11.adv, s32[3]{0:T(128)} %bins.1, s32[3]{0:T(128)} %grps.1, bf16[192,896]{1,0:T(8,128)(2,1)} %wu_in.1, ...), custom_call_target="tpu_custom_call" | custom-call | flops 25367150592 | bytes 8388608 | tf_op jit(solution)/shard_map/block_gradient/pallas_call | solution.py:519
  205.2 0.0 copy-start.1
  205.2 2.4 %copy.15 = f32[768,384]{1,0:T(8,128)} copy(f32[768,384]{1,0:T(8,128)} %get-tuple-element.6) | data formatting | bytes 2359296
  207.6 0.0 copy-done.1
  207.6 0.0 copy-start
  207.6 0.8 copy.16
  208.5 0.5 copy-done
  209.0 0.8 copy.17
Async XLA Ops:
  205.2 2.4 %copy-start.1 = (f32[192,896]{1,0:T(8,128)S(1)}, f32[192,896]{1,0:T(8,128)}, u32[]{:S(2)}) copy-start(f32[192,896]{1,0:T(8,128)} %get-tuple-element.7) | copy-start | bytes 2064388
  207.6 1.3 copy-start

commit v2 on v1

v2 whole, which is shorter than its diff:
```python
import jax
import jax.numpy as jnp
from jax import lax
from jax.experimental import pallas as pl
from jax.experimental.pallas import tpu as pltpu
from jax.sharding import PartitionSpec as P

F32 = jnp.float32
BF16 = jnp.bfloat16
MESH = pl.DeviceIdType.MESH
COEF = 0.7978845608028654


def dot_nn(a, b):
    return jnp.dot(a, b, preferred_element_type=F32)


def dot_nt(a, b):
    return lax.dot_general(a, b, (((1,), (1,)), ((), ())), preferred_element_type=F32)


def dot_tn(a, b):
    return lax.dot_general(a, b, (((0,), (0,)), ((), ())), preferred_element_type=F32)


def gelu_slope(v):
    th = jnp.tanh(COEF * (v + 0.044715 * v * v * v))
    return 0.5 * (1.0 + th) + 0.5 * v * (1.0 - th * th) * COEF * (1.0 + 3 * 0.044715 * v * v)


def tiles(rows, size, body):
    @pl.loop(0, rows // size)
    def _(t):
        body(pl.ds(pl.multiple_of(t * size, size), size))


def make_kernel(rows, feat, depth, hidden, micro, scale):
    seq = rows // micro

    def kernel(
        tok, tgt_in, mod, adv, bins, grps, wu_in, wd_in,
        gt_out, gu_out, gd_out,
        X, Y, Wu, Wd, pre, dh, hid, dpre, SB, RB, SGD, SIBD, SIBU, RGD, RGU, gain,
        tgt, dpred, gt, gu, gd, ss, rs, ls,
    ):
        SGU = Wd
        wi, ni = lax.axis_index("wide"), lax.axis_index("node")
        xh, z, c = wi // 8, (wi // 2) % 4, wi % 2
        xl, y = ni // 4, ni % 4

        def nd(dx, dy):
            return ((xl + dx) % 2) * 4 + (y + dy + 4) % 4

        def wm(dx, dz):
            return ((xh + dx) % 2) * 4 + (z + dz + 4) % 4

        def dnode(dx, dy):
            return (wi, nd(dx, dy))

        def dwide(dx, dz):
            return (wm(dx, dz) * 2 + c, ni)

        sib = (wm(0, 0) * 2 + 1 - c, ni)

        table = {}
        count = [0]

        def add(name, src, dst, got, dev):
            table[name] = (count[0], src, dst, got, dev)
            count[0] += 1

        def desc(name, received):
            i, src, dst, got, dev = table[name]
            return pltpu.make_async_remote_copy(
                src_ref=got if received else src,
                dst_ref=got if received else dst,
                send_sem=ss.at[i],
                recv_sem=rs.at[i],
                device_id=dev,
                device_id_type=MESH,
            )

        def start(*names):
            for name in names:
                desc(name, False).start()

        def recv(*names):
            for name in names:
                desc(name, True).wait_recv()

        def sent(*names):
            for name in names:
                desc(name, False).wait_send()

        part = depth // 16
        mine, other = pl.multiple_of(c * part, part), pl.multiple_of((1 - c) * part, part)
        PC, PS = pl.ds(mine, part), pl.ds(other, part)
        Q1 = pl.ds(mine, part // 2)
        Q2 = pl.ds(pl.multiple_of(mine + part // 2, part // 2), part // 2)
        W = pl.ds(0, rows)
        half = rows // 2
        H1, H2 = pl.ds(0, half), pl.ds(half, half)
        K = [pl.ds(i * (half // 2), half // 2) for i in range(4)]

        def add_ag(p, B, fewer):
            def one(name, blk, r, got, dev):
                add(p + name, B.at[blk, r], B.at[blk, r], B.at[got, r], dev)

            one("yp1", nd(0, 0), H1, nd(0, -1), dnode(0, 1))
            one("yp2", nd(0, 0), H2, nd(0, -1), dnode(0, 1))
            one("ym1", nd(0, 0), H1, nd(0, 1), dnode(0, -1))
            one("ym2", nd(0, 0), H2, nd(0, 1), dnode(0, -1))
            for i, r in (("1", H1), ("2", H2)):
                one("x" + i, nd(0, 0), r, nd(1, 0), dnode(1, 0))
                one("bp" + i, nd(1, 0), r, nd(1, -1), dnode(0, 1))
                one("bm" + i, nd(1, 0), r, nd(1, 1), dnode(0, -1))
            for i, rp, rm in (("1", K[0], K[2]), ("2", K[1], K[3])):
                one("cp" + i, nd(0, -1), rp, nd(0, 2), dnode(0, 1))
                one("cm" + i, nd(0, 1), rm, nd(0, 2), dnode(0, -1))
                one("dp" + i, nd(0, 2), rp, nd(1, 2), dnode(1, 0))
                if not fewer:
                    one("dm" + i, nd(0, 2), rm, nd(1, 2), dnode(1, 0))
            if fewer:
                one("ep", nd(1, -1), K[2], nd(1, 2), dnode(0, 1))
                one("em", nd(1, 1), K[3], nd(1, 2), dnode(0, -1))

        def ag_names(p, fewer):
            names = ["yp", "ym", "x", "bp", "bm", "cp", "cm", "dp"] + ([] if fewer else ["dm"])
            last = ["ep", "em"] if fewer else []
            return [p + n + i for n in names for i in "12"] + [p + n for n in last]

        def add_wag(p, B, b0):
            def one(name, blk, r, got, dev):
                add(p + name, B.at[blk, r], B.at[blk, r], B.at[got, r], dev)

            one("x", wm(0, 0), PC, wm(1, 0), dwide(1, 0))
            for i, b in ((0, b0), (1, 1 - b0)):
                here, up, down, far = (b * 4 + (z + d) % 4 for d in (0, 1, 3, 2))
                one(f"zp{i}", here, Q1, down, dwide(0, 1))
                one(f"zm{i}", here, Q2, up, dwide(0, -1))
                one(f"yp{i}", here, Q2, down, dwide(0, 1))
                one(f"ym{i}", here, Q1, up, dwide(0, -1))
                one(f"cp{i}", down, Q1, far, dwide(0, 1))
                one(f"cm{i}", up, Q2, far, dwide(0, -1))
            base = count[0]
            count[0] += 8

            def share(b, received=False):
                r = PS if received else PC
                return pltpu.make_async_remote_copy(
                    src_ref=B.at[b, r],
                    dst_ref=B.at[b, r],
                    send_sem=ss.at[base + b],
                    recv_sem=rs.at[base + b],
                    device_id=sib,
                    device_id_type=MESH,
                )

            return share

        WAG = ("x",) + tuple(f"{n}{i}" for i in (0, 1) for n in ("zp", "zm", "yp", "ym", "cp", "cm"))

        def add_rs(p, R):
            def one(name, blk, r, slot, dev):
                add(p + name, SB.at[blk, r], R.at[slot, r], R.at[slot, r], dev)

            one("x0", nd(1, 2), W, 0, dnode(1, 0))
            one("bp", nd(1, 1), W, 2, dnode(0, 1))
            one("bm", nd(1, -1), W, 3, dnode(0, -1))
            one("cp", nd(0, 2), H1, 1, dnode(0, 1))
            one("cm", nd(0, 2), H2, 1, dnode(0, -1))
            one("ax", nd(1, 0), W, 4, dnode(1, 0))
            one("ap1", nd(0, 1), H1, 5, dnode(0, 1))
            one("ap2", nd(0, 1), H2, 5, dnode(0, 1))
            one("am1", nd(0, -1), H1, 6, dnode(0, -1))
            one("am2", nd(0, -1), H2, 6, dnode(0, -1))

        RSN = ("x0", "bp", "bm", "cp", "cm", "ax", "ap1", "ap2", "am1", "am2")
        A1, A2 = pl.ds(0, part // 2), pl.ds(part // 2, part // 2)
        AW = pl.ds(0, part)

        def add_wrs(p, S, R, B, b0):
            def one(name, blk, r, slot, rr, dev):
                add(p + name, S.at[blk, r], R.at[slot, rr], R.at[slot, rr], dev)

            one("x", wm(1, 0), PC, 6, AW, dwide(1, 0))
            for i, b in ((0, b0), (1, 1 - b0)):
                up, down, far = (b * 4 + (z + d) % 4 for d in (1, 3, 2))
                one(f"cp{i}", far, Q1, i, A1, dwide(0, 1))
                one(f"cm{i}", far, Q2, i, A2, dwide(0, -1))
                one(f"ap{i}", up, PC, 2 + 2 * i, AW, dwide(0, 1))
                one(f"am{i}", down, PC, 3 + 2 * i, AW, dwide(0, -1))
            base = count[0]
            count[0] += 8

            def share(b):
                return pltpu.make_async_remote_copy(
                    src_ref=S.at[b, PS],
                    dst_ref=B.at[b],
                    send_sem=ss.at[base + b],
                    recv_sem=rs.at[base + b],
                    device_id=sib,
                    device_id_type=MESH,
                )

            return share

        RSW = ("x",) + tuple(f"{n}{i}" for i in (0, 1) for n in ("cp", "cm", "ap", "am"))
        add_ag("X", X, True)
        add_ag("Y", Y, False)
        share_u = add_wag("U", Wu, xh)
        share_d = add_wag("D", Wd, 1 - xl)
        add_rs("P", RB)
        add_rs("M", RB)
        sib_d = add_wrs("G", SGD, RGD, SIBD, xl)
        sib_u = add_wrs("H", SGU, RGU, SIBU, xl)

        barrier = pltpu.get_barrier_semaphore()
        for dev in (dnode(1, 0), dnode(0, 1), dnode(0, -1), dwide(1, 0), dwide(0, 1), dwide(0, -1), sib):
            pl.semaphore_signal(barrier, inc=1, device_id=dev, device_id_type=MESH)
        lu = pltpu.make_async_copy(wu_in, Wu.at[wm(0, 0), PC], ls.at[0])
        ld = pltpu.make_async_copy(wd_in, Wd.at[wm(0, 0), PC], ls.at[1])
        lt = pltpu.make_async_copy(tgt_in, tgt, ls.at[2])
        lu.start()
        ld.start()
        lt.start()

        def back(src, dst, i):
            return pltpu.make_async_copy(src, dst, ls.at[3 + i])

        ng, nb = adv.shape
        row_i = lax.broadcasted_iota(jnp.int32, (nb, feat), 0)
        for s in range(micro):
            picked = jnp.sum(jnp.where(row_i == bins[s], mod[...].astype(F32), 0.0), axis=0, keepdims=True)
            gain[s : s + 1, :] = 1.0 + picked

            def modulate(r, s=s):
                q = pl.ds(pl.multiple_of(r.start + s * seq, 32), r.size)
                X[nd(0, 0), q, :] = (tok[q, :].astype(F32) * gain[s : s + 1, :]).astype(BF16)

            tiles(seq, 32, modulate)
        lu.wait()
        ld.wait()
        pl.semaphore_wait(barrier, 7)

        def ring_start(p, i):
            start(f"{p}zp{i}", f"{p}zm{i}", f"{p}yp{i}", f"{p}ym{i}")

        def ring_relay(p, i):
            recv(f"{p}zp{i}")
            start(f"{p}cp{i}")
            recv(f"{p}zm{i}")
            start(f"{p}cm{i}")

        def ring_share(p, i, b, share):
            recv(f"{p}yp{i}")
            share(b * 4 + (z + 3) % 4).start()
            recv(f"{p}ym{i}")
            share(b * 4 + (z + 1) % 4).start()

        def ring_end(p, i, b, share):
            recv(f"{p}cp{i}", f"{p}cm{i}")
            share(b * 4 + (z + 2) % 4).start()

        same = xh == xl
        start("Xyp1", "Xym2", "Ux")
        ring_start("U", 0)
        start("Xyp2", "Xym1", "Xx2")
        share_u(wm(0, 0)).start()
        share_d(wm(0, 0)).start()

        @pl.when(~same)
        def _():
            start("Dx")

        start("Xx1")

        def zero(r):
            pre[r, :] = jnp.zeros((r.size, hidden), F32)
            dh[r, :] = jnp.zeros((r.size, hidden), F32)

        tiles(rows, 32, zero)
        ring_relay("U", 0)
        recv("Xyp1")
        start("Xcp1", "Xcp2")
        recv("Xym2")
        start("Xcm1", "Xcm2")
        recv("Ux")
        ring_start("U", 1)
        share_u(wm(1, 0)).start()
        ring_share("U", 0, xh, share_u)
        ring_end("U", 0, xh, share_u)
        ring_relay("U", 1)

        @pl.when(~same)
        def _():
            ring_start("D", 0)

        recv("Xx2")
        start("Xbp2", "Xbm2")
        recv("Xcp1", "Xcp2")
        start("Xdp1", "Xdp2")
        recv("Xcm1", "Xcm2")

        @pl.when(same)
        def _():
            start("Dx")
            recv("Dx")
            ring_start("D", 0)
            share_d(wm(1, 0)).start()

        ring_share("U", 1, 1 - xh, share_u)
        ring_end("U", 1, 1 - xh, share_u)
        recv("Xyp2", "Xym1")

        @pl.loop(0, 8)
        def _(b):
            share_u(b, True).wait_recv()

        def arrival(k):
            dx = jnp.where((k == 3) | (k >= 5), 1, 0)
            dy = jnp.where((k == 1) | (k == 5), 1, jnp.where((k == 2) | (k == 6), 3, jnp.where((k == 4) | (k == 7), 2, 0)))
            return ((xl + dx) % 2) * 4 + (y + dy) % 4

        @pl.loop(0, 8)
        def _(k):
            @pl.when(k == 1)
            def _():
                recv("Xx1")
                start("Xbp1", "Xbm1")

            @pl.when(k == 2)
            def _():
                recv("Xbp2")
                start("Xep")
                recv("Xbm2")
                start("Xem")

            @pl.when(k == 5)
            def _():
                ring_relay("D", 0)
                recv("Xbp1", "Xbm1")

            @pl.when(k == 7)
            def _():
                ring_share("D", 0, 1 - xl, share_d)

                @pl.when(~same)
                def _():
                    recv("Dx")
                    share_d(wm(1, 0)).start()

                ring_start("D", 1)
                recv("Xdp1", "Xdp2", "Xep", "Xem")

            n = arrival(k)
            pre[...] += dot_nn(X[n], Wu[n])

        def activate(r):
            hid[r, :] = jax.nn.gelu(pre[r, :], approximate=True).astype(BF16)

        tiles(rows, 32, activate)
        ring_end("D", 0, 1 - xl, share_d)

        def departure(k):
            dx = jnp.where(k <= 3, 1, 0)
            dy = jnp.where((k == 0) | (k == 4), 2, jnp.where((k == 1) | (k == 5), 1, jnp.where((k == 2) | (k == 6), 3, 0)))
            return ((xl + dx) % 2) * 4 + (y + dy) % 4

        def products(p, left, weight, first, last):
            @pl.loop(first, last)
            def _(k):
                n = departure(k)
                SB[n] = dot_nt(left[...], weight[n]).astype(BF16)
                for at, name in ((0, "x0"), (1, "bp"), (2, "bm"), (5, "ap2"), (6, "am1")):
                    if first <= at < last:

                        @pl.when(k == at)
                        def _(name=name):
                            start(p + name)

        def plus(blk, r0, size, R, *slots):
            def body(r):
                q = pl.ds(pl.multiple_of(r.start + r0, 32), r.size)
                v = SB[blk, q, :].astype(F32)
                for slot in slots:
                    v = v + R[slot, q, :].astype(F32)
                SB[blk, q, :] = v.astype(BF16)

            tiles(size, 32, body)

        def rs_first(p, R):
            recv(p + "x0")
            plus(nd(0, 2), 0, rows, R, 0)
            start(p + "cp", p + "cm")

        def rs_second(p, R):
            recv(p + "bp", p + "bm")
            plus(nd(1, 0), 0, rows, R, 2, 3)
            start(p + "ax")

        def rs_third(p, R):
            recv(p + "cp")
            plus(nd(0, 1), 0, half, R, 1)
            start(p + "ap1")
            recv(p + "cm")
            plus(nd(0, -1), half, half, R, 1)
            start(p + "am2")

        def rs_end(p):
            recv(*[p + n for n in ("ax", "ap1", "ap2", "am1", "am2")])

        def wait_column(b, share):
            for d in range(4):
                share(b * 4 + d, True).wait_recv()

        wait_column(1 - xl, share_d)
        products("P", hid, Wd, 0, 4)
        ring_relay("D", 1)
        ring_share("D", 1, xl, share_d)
        ring_end("D", 1, xl, share_d)
        wait_column(xl, share_d)
        products("P", hid, Wd, 4, 5)
        rs_first("P", RB)
        products("P", hid, Wd, 5, 8)
        rs_second("P", RB)
        rs_third("P", RB)
        rs_end("P")
        lt.wait()

        def total(R, q):
            v = SB[nd(0, 0), q, :].astype(F32) + R[4, q, :].astype(F32)
            return v + R[5, q, :].astype(F32) + R[6, q, :].astype(F32)

        bin_i = lax.broadcasted_iota(jnp.int32, (ng, nb), 1)
        grp_i = lax.broadcasted_iota(jnp.int32, (ng, nb), 0)
        for s in range(micro):
            chosen = jnp.where((bin_i == bins[s]) & (grp_i == grps[s]), adv[...], 0.0)
            weight = jnp.sum(jnp.sum(chosen, axis=1, keepdims=True), axis=0, keepdims=True)

            def error(r, s=s, weight=weight):
                q = pl.ds(pl.multiple_of(r.start + s * seq, 32), r.size)
                d = weight * (tok[q, :].astype(F32) + total(RB, q) - tgt[q, :].astype(F32))
                dpred[q, :] = d
                Y[nd(0, 0), q, :] = d.astype(BF16)

            tiles(seq, 32, error)

        start("Yyp1", "Yym2", "Yx1", "Yx2", "Yyp2", "Yym1")
        sent(*["P" + n for n in RSN])

        def stage_down(m):
            SGD[m] = (dot_tn(Y[m], hid[...]) * scale).astype(BF16)
            sib_d(m).start()

        def stage_up(m):
            SGU[m] = (dot_tn(X[m], dpre[...]) * scale).astype(BF16)
            sib_u(m).start()

        def wide_plus(S, blk, slots, r0, size):
            def body(r):
                a = pl.ds(pl.multiple_of(r.start + r0, 32), r.size)
                q = pl.ds(pl.multiple_of(mine + r.start + r0, 32), r.size)
                v = S[blk, q, :].astype(F32)
                for ref, slot in slots:
                    v = v + ref[slot, a, :].astype(F32)
                S[blk, q, :] = v.astype(BF16)

            tiles(size, 32, body)

        quarter = part // 2

        def wide_first(p, i, b, S, B, share):
            m = b * 4 + (z + 2) % 4
            share(m).wait_recv()
            wide_plus(S, m, ((B, m),), 0, part)
            start(f"{p}cp{i}", f"{p}cm{i}")

        def wide_second(p, i, b, S, B, R, share):
            for d in (1, 3, 0):
                share(b * 4 + (z + d) % 4).wait_recv()
            m = b * 4 + (z + 1) % 4
            wide_plus(S, m, ((B, m),), quarter, quarter)
            recv(f"{p}cp{i}")
            wide_plus(S, m, ((B, m), (R, i)), 0, quarter)
            start(f"{p}ap{i}")
            m = b * 4 + (z + 3) % 4
            wide_plus(S, m, ((B, m),), 0, quarter)
            recv(f"{p}cm{i}")
            wide_plus(S, m, ((B, m), (R, i)), quarter, quarter)
            start(f"{p}am{i}")

        def wide_third(p, i, b, S, B, R):
            recv(f"{p}ap{i}", f"{p}am{i}")

            @pl.when(xh != b)
            def _():
                m = b * 4 + z
                wide_plus(S, m, ((B, m), (R, 2 + 2 * i), (R, 3 + 2 * i)), 0, part)
                start(p + "x")

        def wide_last(p, b0, S, B, R, out):
            recv(p + "x")
            m = wm(0, 0)
            slot = jnp.where(xh == b0, 2, 4)

            def body(r):
                q = pl.ds(pl.multiple_of(mine + r.start, 32), r.size)
                v = S[m, q, :].astype(F32) + B[m, r, :].astype(F32)
                v = v + R[slot, r, :].astype(F32) + R[slot + 1, r, :].astype(F32)
                out[r, :] = (v + R[6, r, :].astype(F32)).astype(BF16)

            tiles(part, 32, body)

        G0 = ("G", 0, xl, SGD, SIBD)
        G1 = ("G", 1, 1 - xl, SGD, SIBD)
        U0 = ("H", 0, xl, SGU, SIBU)
        U1 = ("H", 1, 1 - xl, SGU, SIBU)

        @pl.loop(0, 5)
        def _(k):
            @pl.when(k == 1)
            def _():
                recv("Yyp1")
                start("Ycp1", "Ycp2")
                recv("Yym2")
                start("Ycm1", "Ycm2")
                recv("Yx1")
                start("Ybp1", "Ybm1")
                recv("Yx2")
                start("Ybp2", "Ybm2")
                recv("Yyp2", "Yym1")

            @pl.when(k == 4)
            def _():
                for i in "12":
                    recv("Ycp" + i)
                    start("Ydp" + i)
                    recv("Ycm" + i)
                    start("Ydm" + i)

            n = arrival(k)

            @pl.when(k != 3)
            def _():
                stage_down(n)

            dh[...] += dot_nn(Y[n], Wd[n])

        wide_first(*G0, sib_d)
        wide_second(*G0, RGD, sib_d)
        recv(*["Y" + n + i for n in ("bp", "bm", "dp", "dm") for i in "12"])
        stage_down((1 - xl) * 4 + (z + 2) % 4)

        @pl.loop(5, 8)
        def _(k):
            n = arrival(k)
            dh[...] += dot_nn(Y[n], Wd[n])

        wide_first(*G1, sib_d)

        def slope(r):
            dpre[r, :] = (dh[r, :] * gelu_slope(pre[r, :])).astype(BF16)

        tiles(rows, 32, slope)

        products("M", dpre, Wu, 0, 3)
        sent(*["D" + n for n in WAG])

        @pl.loop(0, 8)
        def _(b):
            share_d(b).wait_send()

        @pl.loop(0, 2)
        def _(k):
            stage_up(((xl + k) % 2) * 4 + (z + 2) % 4)

        wide_first(*U0, sib_u)
        wide_first(*U1, sib_u)

        @pl.loop(0, 3)
        def _(k):
            stage_down((1 - xl) * 4 + (z + 3 + k) % 4)

        wide_second(*G1, RGD, sib_d)
        wide_third("G", 0, xl, SGD, SIBD, RGD)
        products("M", dpre, Wu, 3, 5)

        @pl.loop(0, 3)
        def _(k):
            stage_up(xl * 4 + (z + 3 + k) % 4)

        rs_first("M", RB)
        rs_second("M", RB)
        wide_second(*U0, RGU, sib_u)
        products("M", dpre, Wu, 5, 8)

        @pl.loop(0, 3)
        def _(k):
            stage_up((1 - xl) * 4 + (z + 3 + k) % 4)

        rs_third("M", RB)
        wide_second(*U1, RGU, sib_u)
        wide_third("G", 1, 1 - xl, SGD, SIBD, RGD)
        wide_third("H", 0, xl, SGU, SIBU, RGU)
        rs_end("M")
        for s in range(micro):

            def finish(r, s=s):
                q = pl.ds(pl.multiple_of(r.start + s * seq, 32), r.size)
                gt[q, :] = (dpred[q, :] + gain[s : s + 1, :] * total(RB, q)).astype(BF16)

            tiles(seq, 32, finish)
        back(gt, gt_out, 1).start()
        wide_last("G", xl, SGD, SIBD, RGD, gd)
        back(gd, gd_out, 0).start()
        wide_third("H", 1, 1 - xl, SGU, SIBU, RGU)
        wide_last("H", xl, SGU, SIBU, RGU, gu)
        back(gu, gu_out, 2).start()

        sent(*ag_names("X", True), *ag_names("Y", False), *["U" + n for n in WAG], *["M" + n for n in RSN])
        sent(*["G" + n for n in RSW], *["H" + n for n in RSW])

        @pl.loop(0, 8)
        def _(b):
            share_u(b).wait_send()
            sib_d(b).wait_send()
            sib_u(b).wait_send()

        back(gd, gd_out, 0).wait()
        back(gt, gt_out, 1).wait()
        back(gu, gu_out, 2).wait()

    return kernel


TRANSFERS = 18 + 18 + 21 * 2 + 10 * 2 + 17 * 2


def on_device(tokens, target, mod_table, adv_table, w_up, w_down_t, bins, groups):
    rows, feat = tokens.shape
    part, hidden = w_up.shape
    depth = part * 16
    micro = bins.shape[0]
    scale = float(16 * rows) ** (-0.5)
    vmem = pl.BlockSpec(memory_space=pltpu.VMEM)
    smem = pl.BlockSpec(memory_space=pltpu.SMEM)
    anys = pl.BlockSpec(memory_space=pl.ANY)
    block = (8, rows, feat)
    wblock = (8, depth // 8, hidden)
    V = pltpu.VMEM
    flops = 6 * 2 * rows * depth * hidden
    grads = pl.pallas_call(
        make_kernel(rows, feat, depth, hidden, micro, scale),
        out_shape=(
            jax.ShapeDtypeStruct((rows, feat), BF16),
            jax.ShapeDtypeStruct((part, hidden), BF16),
            jax.ShapeDtypeStruct((part, hidden), BF16),
        ),
        in_specs=[vmem, anys, vmem, vmem, smem, smem, anys, anys],
        out_specs=(anys, anys, anys),
        scratch_shapes=[
            V(block, BF16), V(block, BF16), V(wblock, BF16), V(wblock, BF16),
            V((rows, hidden), F32), V((rows, hidden), F32), V((rows, hidden), BF16), V((rows, hidden), BF16),
            V(block, BF16), V((7, rows, feat), BF16),
            V(wblock, BF16), V((8, part, hidden), BF16), V((8, part, hidden), BF16),
            V((7, part, hidden), BF16), V((7, part, hidden), BF16),
            V((8, feat), F32),
            V((rows, feat), BF16), V((rows, feat), F32), V((rows, feat), BF16), V((part, hidden), BF16), V((part, hidden), BF16),
            pltpu.SemaphoreType.DMA((TRANSFERS,)),
            pltpu.SemaphoreType.DMA((TRANSFERS,)),
            pltpu.SemaphoreType.DMA((6,)),
        ],
        compiler_params=pltpu.CompilerParams(
            collective_id=0, has_side_effects=True, vmem_limit_bytes=63 * 2**20
        ),
        cost_estimate=pl.CostEstimate(flops=flops, bytes_accessed=8 * 2**20, transcendentals=2 * rows * hidden),
        name="block_gradient",
    )(tokens, target, mod_table, adv_table.T, bins, groups, w_up, w_down_t)
    return tuple(g.astype(F32) for g in grads)


def solution(mesh):
    return jax.shard_map(
        on_device,
        mesh=mesh,
        in_specs=(
            P("wide", "node"),
            P("wide", "node"),
            P(None, "node"),
            P(),
            P("wide", "node"),
            P("wide", "node"),
            P("wide"),
            P("wide"),
        ),
        out_specs=(P("wide", "node"), P("wide", "node"), P("wide", "node")),
        check_vma=False,
    )
```

time: 212 us -> 184 us (0.87); the launches traced: 210 us -> 184 us
  Pallas kernels: 203 us -> 179 us
  local copies, waits for them, and re-layouts: 6 us -> 0.01 us
  other arithmetic: 0 us -> 4.01 us
    pallas_call x1, Pallas kernels: 203 us -> 179 us  [on_device(): pl.pallas_call(make_kernel(rows, feat, depth, hidden, micro, scale), out_...]
    unnamed x8 -> x4, local copies, waits for them, and re-layouts: 6 us -> 0.01 us
    convert_element_type x0 -> x3, other arithmetic: none -> 4.01 us  [on_device(): return tuple((g.astype(F32) for g in grads))]
where the time goes in v2:
time: 184 us
  Pallas kernels  179 us (97%)
  other arithmetic  4.01 us (2%)
    pallas_call x1, Pallas kernels, on_device(): pl.pallas_call(make_kernel(rows, feat, depth, hidden, micro, scale), out_...  179 us
    convert_element_type x3, other arithmetic, on_device(): return tuple((g.astype(F32) for g in grads))  4.01 us

profile of v2, /device:TPU:2, one launch (start us, length us, event | category | flops | bytes accessed | tf_op | source)
XLA Modules:
  0.0 184.0 jit_solution(2491978168890607425)
XLA Ops:
  0.6 179.3 %block_gradient.1 = (bf16[768,384]{1,0:T(8,128)(2,1)}, bf16[192,896]{1,0:T(8,128)(2,1)}, bf16[192,896]{1,0:T(8,128)(2,1)}) custom-call(bf16[768,384]{1,0:T(8,128)(2,1)} %tok.1, bf16[768,384]{1,0:T(8,128)(2,1)} %tgt_in.1, bf16[32,384]{1,0:T(8,128)(2,1)} %mod.1, f32[16,32]{1,0:T(8,128)} %bitcast.1, s32[3]{0:T(128)} %bins.1, s32[3]{0:T(128)} %grps.1, ...), custom_call_target="tpu_custom_call" | custom-call | flops 25367150592 | bytes 8388608 | tf_op jit(solution)/shard_map/block_gradient/pallas_call | solution.py:653
  179.9 0.0 copy-start.1
  179.9 0.0 copy-start
  179.9 2.2 %convert_element_type.9 = f32[768,384]{1,0:T(8,128)} convert(bf16[768,384]{1,0:T(8,128)(2,1)} %get-tuple-element.6) | non-fusion elementwise | flops 294912 | bytes 1769472 | tf_op jit(solution)/shard_map/convert_element_type | solution.py:680
  182.2 0.0 copy-done.1
  182.2 0.9 convert_element_type.10
  183.1 0.0 copy-done
  183.1 0.9 convert_element_type.11
Async XLA Ops:
  179.9 2.2 %copy-start.1 = (bf16[192,896]{1,0:T(8,128)(2,1)S(1)}, bf16[192,896]{1,0:T(8,128)(2,1)}, u32[]{:S(2)}) copy-start(bf16[192,896]{1,0:T(8,128)(2,1)} %get-tuple-element.7) | copy-start | bytes 1032196
  179.9 3.1 %copy-start = (bf16[192,896]{1,0:T(8,128)(2,1)S(1)}, bf16[192,896]{1,0:T(8,128)(2,1)}, u32[]{:S(2)}) copy-start(bf16[192,896]{1,0:T(8,128)(2,1)} %get-tuple-element.8) | copy-start | bytes 1032196

commit v3 on v2

--- a/solution.py
+++ b/solution.py
@@ -38,10 +38,10 @@
     seq = rows // micro
 
     def kernel(
-        tok, tgt_in, mod, adv, bins, grps, wu_in, wd_in,
+        tok_in, tgt_in, mod_in, adv_in, bins_in, grps_in, wu_in, wd_in,
         gt_out, gu_out, gd_out,
         X, Y, Wu, Wd, pre, dh, hid, dpre, SB, RB, SGD, SIBD, SIBU, RGD, RGU, gain,
-        tgt, dpred, gt, gu, gd, ss, rs, ls,
+        bins, grps, tok, mod, adv, tgt, dpred, gt, gu, gd, ss, rs, ls,
     ):
         SGU = Wd
         wi, ni = lax.axis_index("wide"), lax.axis_index("node")
@@ -106,10 +106,9 @@
             def one(name, blk, r, got, dev):
                 add(p + name, B.at[blk, r], B.at[blk, r], B.at[got, r], dev)
 
-            one("yp1", nd(0, 0), H1, nd(0, -1), dnode(0, 1))
-            one("yp2", nd(0, 0), H2, nd(0, -1), dnode(0, 1))
-            one("ym1", nd(0, 0), H1, nd(0, 1), dnode(0, -1))
-            one("ym2", nd(0, 0), H2, nd(0, 1), dnode(0, -1))
+            for i, rp, rm in (("1", K[0], K[2]), ("2", K[1], K[3]), ("3", H2, H1)):
+                one("yp" + i, nd(0, 0), rp, nd(0, -1), dnode(0, 1))
+                one("ym" + i, nd(0, 0), rm, nd(0, 1), dnode(0, -1))
             for i, r in (("1", H1), ("2", H2)):
                 one("x" + i, nd(0, 0), r, nd(1, 0), dnode(1, 0))
                 one("bp" + i, nd(1, 0), r, nd(1, -1), dnode(0, 1))
@@ -126,7 +125,7 @@
 
         def ag_names(p, fewer):
             names = ["yp", "ym", "x", "bp", "bm", "cp", "cm", "dp"] + ([] if fewer else ["dm"])
-            last = ["ep", "em"] if fewer else []
+            last = ["yp3", "ym3"] + (["ep", "em"] if fewer else [])
             return [p + n + i for n in names for i in "12"] + [p + n for n in last]
 
         def add_wag(p, B, b0):
@@ -164,18 +163,19 @@
             def one(name, blk, r, slot, dev):
                 add(p + name, SB.at[blk, r], R.at[slot, r], R.at[slot, r], dev)
 
-            one("x0", nd(1, 2), W, 0, dnode(1, 0))
-            one("bp", nd(1, 1), W, 2, dnode(0, 1))
-            one("bm", nd(1, -1), W, 3, dnode(0, -1))
-            one("cp", nd(0, 2), H1, 1, dnode(0, 1))
-            one("cm", nd(0, 2), H2, 1, dnode(0, -1))
+            for i, r in (("1", H1), ("2", H2)):
+                one("x" + i, nd(1, 2), r, 0, dnode(1, 0))
+                one("bp" + i, nd(1, 1), r, 2, dnode(0, 1))
+                one("bm" + i, nd(1, -1), r, 3, dnode(0, -1))
             one("ax", nd(1, 0), W, 4, dnode(1, 0))
-            one("ap1", nd(0, 1), H1, 5, dnode(0, 1))
-            one("ap2", nd(0, 1), H2, 5, dnode(0, 1))
-            one("am1", nd(0, -1), H1, 6, dnode(0, -1))
-            one("am2", nd(0, -1), H2, 6, dnode(0, -1))
-
-        RSN = ("x0", "bp", "bm", "cp", "cm", "ax", "ap1", "ap2", "am1", "am2")
+            for i, rp, rm in (("1", K[0], K[2]), ("2", K[1], K[3])):
+                one("cp" + i, nd(0, 2), rp, 1, dnode(0, 1))
+                one("cm" + i, nd(0, 2), rm, 1, dnode(0, -1))
+            for i, rp, rm in (("1", K[0], K[2]), ("2", K[1], K[3]), ("3", H2, H1)):
+                one("ap" + i, nd(0, 1), rp, 5, dnode(0, 1))
+                one("am" + i, nd(0, -1), rm, 6, dnode(0, -1))
+
+        RSN = ["ax"] + [n + i for n in ("x", "bp", "bm", "cp", "cm", "ap", "am") for i in "12"] + ["ap3", "am3"]
         A1, A2 = pl.ds(0, part // 2), pl.ds(part // 2, part // 2)
         AW = pl.ds(0, part)
 
@@ -183,13 +183,15 @@
             def one(name, blk, r, slot, rr, dev):
                 add(p + name, S.at[blk, r], R.at[slot, rr], R.at[slot, rr], dev)
 
-            one("x", wm(1, 0), PC, 6, AW, dwide(1, 0))
+            one("xa", wm(1, 0), Q1, 6, A1, dwide(1, 0))
+            one("xb", wm(1, 0), Q2, 6, A2, dwide(1, 0))
             for i, b in ((0, b0), (1, 1 - b0)):
                 up, down, far = (b * 4 + (z + d) % 4 for d in (1, 3, 2))
                 one(f"cp{i}", far, Q1, i, A1, dwide(0, 1))
                 one(f"cm{i}", far, Q2, i, A2, dwide(0, -1))
-                one(f"ap{i}", up, PC, 2 + 2 * i, AW, dwide(0, 1))
-                one(f"am{i}", down, PC, 3 + 2 * i, AW, dwide(0, -1))
+                for h, r, a in (("a", Q1, A1), ("b", Q2, A2)):
+                    one(f"ap{i}{h}", up, r, 2 + 2 * i, a, dwide(0, 1))
+                    one(f"am{i}{h}", down, r, 3 + 2 * i, a, dwide(0, -1))
             base = count[0]
             count[0] += 8
 
@@ -205,7 +207,7 @@
 
             return share
 
-        RSW = ("x",) + tuple(f"{n}{i}" for i in (0, 1) for n in ("cp", "cm", "ap", "am"))
+        RSW = ("xa", "xb") + tuple(n.format(i) for i in (0, 1) for n in ("cp{}", "cm{}", "ap{}a", "ap{}b", "am{}a", "am{}b"))
         add_ag("X", X, True)
         add_ag("Y", Y, False)
         share_u = add_wag("U", Wu, xh)
@@ -221,6 +223,16 @@
         lu = pltpu.make_async_copy(wu_in, Wu.at[wm(0, 0), PC], ls.at[0])
         ld = pltpu.make_async_copy(wd_in, Wd.at[wm(0, 0), PC], ls.at[1])
         lt = pltpu.make_async_copy(tgt_in, tgt, ls.at[2])
+        lk = pltpu.make_async_copy(tok_in, tok, ls.at[6])
+        lm = pltpu.make_async_copy(mod_in, mod, ls.at[7])
+        la = pltpu.make_async_copy(adv_in, adv, ls.at[8])
+        lb = pltpu.make_async_copy(bins_in, bins, ls.at[9])
+        lg = pltpu.make_async_copy(grps_in, grps, ls.at[10])
+        lb.start()
+        lg.start()
+        lm.start()
+        lk.start()
+        la.start()
         lu.start()
         ld.start()
         lt.start()
@@ -229,6 +241,10 @@
             return pltpu.make_async_copy(src, dst, ls.at[3 + i])
 
         ng, nb = adv.shape
+        lb.wait()
+        lg.wait()
+        lm.wait()
+        lk.wait()
         row_i = lax.broadcasted_iota(jnp.int32, (nb, feat), 0)
         for s in range(micro):
             picked = jnp.sum(jnp.where(row_i == bins[s], mod[...].astype(F32), 0.0), axis=0, keepdims=True)
@@ -263,9 +279,9 @@
             share(b * 4 + (z + 2) % 4).start()
 
         same = xh == xl
-        start("Xyp1", "Xym2", "Ux")
+        start("Xyp1", "Xym1", "Xyp2", "Xym2", "Ux")
         ring_start("U", 0)
-        start("Xyp2", "Xym1", "Xx2")
+        start("Xyp3", "Xym3")
         share_u(wm(0, 0)).start()
         share_d(wm(0, 0)).start()
 
@@ -273,7 +289,7 @@
         def _():
             start("Dx")
 
-        start("Xx1")
+        start("Xx2", "Xx1")
 
         def zero(r):
             pre[r, :] = jnp.zeros((r.size, hidden), F32)
@@ -281,10 +297,12 @@
 
         tiles(rows, 32, zero)
         ring_relay("U", 0)
-        recv("Xyp1")
-        start("Xcp1", "Xcp2")
-        recv("Xym2")
-        start("Xcm1", "Xcm2")
+        def far_relay(p):
+            for d in ("p1", "m1", "p2", "m2"):
+                recv(p + "y" + d)
+                start(p + "c" + d)
+
+        far_relay("X")
         recv("Ux")
         ring_start("U", 1)
         share_u(wm(1, 0)).start()
@@ -292,10 +310,12 @@
         ring_end("U", 0, xh, share_u)
         ring_relay("U", 1)
 
-        @pl.when(~same)
+        @pl.when(same)
         def _():
-            ring_start("D", 0)
-
+            recv("Dx")
+            share_d(wm(1, 0)).start()
+
+        ring_start("D", 0)
         recv("Xx2")
         start("Xbp2", "Xbm2")
         recv("Xcp1", "Xcp2")
@@ -305,13 +325,10 @@
         @pl.when(same)
         def _():
             start("Dx")
-            recv("Dx")
-            ring_start("D", 0)
-            share_d(wm(1, 0)).start()
 
         ring_share("U", 1, 1 - xh, share_u)
         ring_end("U", 1, 1 - xh, share_u)
-        recv("Xyp2", "Xym1")
+        recv("Xyp3", "Xym3")
 
         @pl.loop(0, 8)
         def _(b):
@@ -322,7 +339,7 @@
             dy = jnp.where((k == 1) | (k == 5), 1, jnp.where((k == 2) | (k == 6), 3, jnp.where((k == 4) | (k == 7), 2, 0)))
             return ((xl + dx) % 2) * 4 + (y + dy) % 4
 
-        @pl.loop(0, 8)
+        @pl.loop(0, 5)
         def _(k):
             @pl.when(k == 1)
             def _():
@@ -336,43 +353,59 @@
                 recv("Xbm2")
                 start("Xem")
 
-            @pl.when(k == 5)
-            def _():
-                ring_relay("D", 0)
-                recv("Xbp1", "Xbm1")
-
-            @pl.when(k == 7)
-            def _():
-                ring_share("D", 0, 1 - xl, share_d)
-
-                @pl.when(~same)
-                def _():
-                    recv("Dx")
-                    share_d(wm(1, 0)).start()
-
-                ring_start("D", 1)
-                recv("Xdp1", "Xdp2", "Xep", "Xem")
-
             n = arrival(k)
             pre[...] += dot_nn(X[n], Wu[n])
 
-        def activate(r):
-            hid[r, :] = jax.nn.gelu(pre[r, :], approximate=True).astype(BF16)
-
-        tiles(rows, 32, activate)
-        ring_end("D", 0, 1 - xl, share_d)
+        ring_relay("D", 0)
+        ring_share("D", 0, 1 - xl, share_d)
+
+        @pl.when(same)
+        def _():
+            ring_start("D", 1)
+
+        def forward(i, r):
+            if i == "1":
+                recv("Xbp1", "Xbm1", "Xdp1", "Xdp2")
+            else:
+                recv("Xep", "Xem")
+
+            @pl.loop(5, 8)
+            def _(k):
+                n = arrival(k)
+                pre[r] += dot_nn(X[n, r], Wu[n])
+
+            def activate(t):
+                q = pl.ds(pl.multiple_of(t.start + r.start, 32), t.size)
+                hid[q, :] = jax.nn.gelu(pre[q, :], approximate=True).astype(BF16)
+
+            if i == "1":
+                ring_end("D", 0, 1 - xl, share_d)
+            tiles(r.size, 32, activate)
+            if i == "1":
+                wait_column(1 - xl, share_d)
+            products("P", hid, Wd, 0, 3, r)
 
         def departure(k):
             dx = jnp.where(k <= 3, 1, 0)
             dy = jnp.where((k == 0) | (k == 4), 2, jnp.where((k == 1) | (k == 5), 1, jnp.where((k == 2) | (k == 6), 3, 0)))
             return ((xl + dx) % 2) * 4 + (y + dy) % 4
 
-        def products(p, left, weight, first, last):
+        def products(p, left, weight, first, last, r=W):
             @pl.loop(first, last)
             def _(k):
                 n = departure(k)
-                SB[n] = dot_nt(left[...], weight[n]).astype(BF16)
-                for at, name in ((0, "x0"), (1, "bp"), (2, "bm"), (5, "ap2"), (6, "am1")):
+                SB[n, r] = dot_nt(left[r], weight[n]).astype(BF16)
+                for at, name in ((0, "x"), (1, "bp"), (2, "bm")):
+                    if first <= at < last:
+
+                        @pl.when(k == at)
+                        def _(name=name):
+                            if r.start == 0:
+                                start(p + name + "1")
+                            if r.start + r.size == rows:
+                                start(p + name + "2")
+
+                for at, name in ((5, "ap3"), (6, "am3")):
                     if first <= at < last:
 
                         @pl.when(k == at)
@@ -390,32 +423,46 @@
             tiles(size, 32, body)
 
         def rs_first(p, R):
-            recv(p + "x0")
-            plus(nd(0, 2), 0, rows, R, 0)
-            start(p + "cp", p + "cm")
+            recv(p + "x1")
+            plus(nd(0, 2), 0, half, R, 0)
+            start(p + "cp1", p + "cp2")
+            recv(p + "x2")
+            plus(nd(0, 2), half, half, R, 0)
+            start(p + "cm1", p + "cm2")
 
         def rs_second(p, R):
-            recv(p + "bp", p + "bm")
+            recv(*[p + n + i for i in "12" for n in ("bp", "bm")])
             plus(nd(1, 0), 0, rows, R, 2, 3)
             start(p + "ax")
 
         def rs_third(p, R):
-            recv(p + "cp")
-            plus(nd(0, 1), 0, half, R, 1)
-            start(p + "ap1")
-            recv(p + "cm")
-            plus(nd(0, -1), half, half, R, 1)
-            start(p + "am2")
-
-        def rs_end(p):
-            recv(*[p + n for n in ("ax", "ap1", "ap2", "am1", "am2")])
+            for i, r in ((1, 0), (2, 1)):
+                recv(f"{p}cp{i}")
+                plus(nd(0, 1), K[r].start, half // 2, R, 1)
+                start(f"{p}ap{i}")
+                recv(f"{p}cm{i}")
+                plus(nd(0, -1), K[r + 2].start, half // 2, R, 1)
+                start(f"{p}am{i}")
+
+        def rs_end(p, i):
+            if i == 1:
+                recv(p + "ax", p + "ap3", p + "am3")
+            recv(f"{p}ap{i}", f"{p}am{i}")
 
         def wait_column(b, share):
             for d in range(4):
                 share(b * 4 + d, True).wait_recv()
 
-        wait_column(1 - xl, share_d)
-        products("P", hid, Wd, 0, 4)
+        forward("1", H1)
+
+        @pl.when(~same)
+        def _():
+            recv("Dx")
+            share_d(wm(1, 0)).start()
+            ring_start("D", 1)
+
+        forward("2", H2)
+        products("P", hid, Wd, 3, 4)
         ring_relay("D", 1)
         ring_share("D", 1, xl, share_d)
         ring_end("D", 1, xl, share_d)
@@ -425,8 +472,9 @@
         products("P", hid, Wd, 5, 8)
         rs_second("P", RB)
         rs_third("P", RB)
-        rs_end("P")
+        rs_end("P", 1)
         lt.wait()
+        la.wait()
 
         def total(R, q):
             v = SB[nd(0, 0), q, :].astype(F32) + R[4, q, :].astype(F32)
@@ -434,19 +482,32 @@
 
         bin_i = lax.broadcasted_iota(jnp.int32, (ng, nb), 1)
         grp_i = lax.broadcasted_iota(jnp.int32, (ng, nb), 0)
+        weight = []
         for s in range(micro):
             chosen = jnp.where((bin_i == bins[s]) & (grp_i == grps[s]), adv[...], 0.0)
-            weight = jnp.sum(jnp.sum(chosen, axis=1, keepdims=True), axis=0, keepdims=True)
-
-            def error(r, s=s, weight=weight):
-                q = pl.ds(pl.multiple_of(r.start + s * seq, 32), r.size)
-                d = weight * (tok[q, :].astype(F32) + total(RB, q) - tgt[q, :].astype(F32))
-                dpred[q, :] = d
-                Y[nd(0, 0), q, :] = d.astype(BF16)
-
-            tiles(seq, 32, error)
-
-        start("Yyp1", "Yym2", "Yx1", "Yx2", "Yyp2", "Yym1")
+            weight.append(jnp.sum(jnp.sum(chosen, axis=1, keepdims=True), axis=0, keepdims=True))
+
+        def error(k):
+            begin, end = K[k].start, K[k].start + K[k].size
+            for s in range(micro):
+                lo, hi = max(begin, s * seq), min(end, (s + 1) * seq)
+
+                def body(r, s=s, lo=lo):
+                    q = pl.ds(pl.multiple_of(r.start + lo, 32), r.size)
+                    d = weight[s] * (tok[q, :].astype(F32) + total(RB, q) - tgt[q, :].astype(F32))
+                    dpred[q, :] = d
+                    Y[nd(0, 0), q, :] = d.astype(BF16)
+
+                if lo < hi:
+                    tiles(hi - lo, 32, body)
+
+        error(0)
+        error(2)
+        start("Yyp1", "Yym1")
+        rs_end("P", 2)
+        error(1)
+        error(3)
+        start("Yyp2", "Yym2", "Yx1", "Yx2", "Yyp3", "Yym3")
         sent(*["P" + n for n in RSN])
 
         def stage_down(m):
@@ -476,31 +537,52 @@
             wide_plus(S, m, ((B, m),), 0, part)
             start(f"{p}cp{i}", f"{p}cm{i}")
 
+        def wide_early(p, i, b, S, B, share):
+            up, down = b * 4 + (z + 1) % 4, b * 4 + (z + 3) % 4
+            share(up).wait_recv()
+            wide_plus(S, up, ((B, up),), quarter, quarter)
+            start(f"{p}ap{i}b")
+            share(down).wait_recv()
+            wide_plus(S, down, ((B, down),), 0, quarter)
+            start(f"{p}am{i}a")
+
         def wide_second(p, i, b, S, B, R, share):
-            for d in (1, 3, 0):
-                share(b * 4 + (z + d) % 4).wait_recv()
-            m = b * 4 + (z + 1) % 4
-            wide_plus(S, m, ((B, m),), quarter, quarter)
+            up, down = b * 4 + (z + 1) % 4, b * 4 + (z + 3) % 4
             recv(f"{p}cp{i}")
-            wide_plus(S, m, ((B, m), (R, i)), 0, quarter)
-            start(f"{p}ap{i}")
-            m = b * 4 + (z + 3) % 4
-            wide_plus(S, m, ((B, m),), 0, quarter)
+            wide_plus(S, up, ((B, up), (R, i)), 0, quarter)
+            start(f"{p}ap{i}a")
             recv(f"{p}cm{i}")
-            wide_plus(S, m, ((B, m), (R, i)), quarter, quarter)
-            start(f"{p}am{i}")
+            wide_plus(S, down, ((B, down), (R, i)), quarter, quarter)
+            start(f"{p}am{i}b")
+            share(b * 4 + z).wait_recv()
+
+        def wide_step(p, i, b, S, B, R, share):
+            up, down = b * 4 + (z + 1) % 4, b * 4 + (z + 3) % 4
+            recv(f"{p}cp{i}", f"{p}cm{i}")
+            share(up).wait_recv()
+            wide_plus(S, up, ((B, up), (R, i)), 0, quarter)
+            start(f"{p}ap{i}a")
+            share(down).wait_recv()
+            wide_plus(S, down, ((B, down),), 0, quarter)
+            start(f"{p}am{i}a")
+            wide_plus(S, up, ((B, up),), quarter, quarter)
+            start(f"{p}ap{i}b")
+            wide_plus(S, down, ((B, down), (R, i)), quarter, quarter)
+            start(f"{p}am{i}b")
+            share(b * 4 + z).wait_recv()
 
         def wide_third(p, i, b, S, B, R):
-            recv(f"{p}ap{i}", f"{p}am{i}")
-
-            @pl.when(xh != b)
-            def _():
-                m = b * 4 + z
-                wide_plus(S, m, ((B, m), (R, 2 + 2 * i), (R, 3 + 2 * i)), 0, part)
-                start(p + "x")
+            m = b * 4 + z
+            for h, r0 in (("a", 0), ("b", quarter)):
+                recv(f"{p}ap{i}{h}", f"{p}am{i}{h}")
+
+                @pl.when(xh != b)
+                def _(h=h, r0=r0):
+                    wide_plus(S, m, ((B, m), (R, 2 + 2 * i), (R, 3 + 2 * i)), r0, quarter)
+                    start(p + "x" + h)
 
         def wide_last(p, b0, S, B, R, out):
-            recv(p + "x")
+            recv(p + "xa", p + "xb")
             m = wm(0, 0)
             slot = jnp.where(xh == b0, 2, 4)
 
@@ -521,23 +603,18 @@
         def _(k):
             @pl.when(k == 1)
             def _():
-                recv("Yyp1")
-                start("Ycp1", "Ycp2")
-                recv("Yym2")
-                start("Ycm1", "Ycm2")
+                far_relay("Y")
                 recv("Yx1")
                 start("Ybp1", "Ybm1")
                 recv("Yx2")
                 start("Ybp2", "Ybm2")
-                recv("Yyp2", "Yym1")
+                recv("Yyp3", "Yym3")
 
             @pl.when(k == 4)
             def _():
-                for i in "12":
-                    recv("Ycp" + i)
-                    start("Ydp" + i)
-                    recv("Ycm" + i)
-                    start("Ydm" + i)
+                for d in ("p1", "p2", "m1", "m2"):
+                    recv("Yc" + d)
+                    start("Yd" + d)
 
             n = arrival(k)
 
@@ -545,65 +622,86 @@
             def _():
                 stage_down(n)
 
-            dh[...] += dot_nn(Y[n], Wd[n])
+            @pl.when(k != 4)
+            def _():
+                dh[...] += dot_nn(Y[n], Wd[n])
 
         wide_first(*G0, sib_d)
+        wide_early(*G0, sib_d)
+        last = arrival(4)
+        dh[...] += dot_nn(Y[last], Wd[last])
         wide_second(*G0, RGD, sib_d)
-        recv(*["Y" + n + i for n in ("bp", "bm", "dp", "dm") for i in "12"])
-        stage_down((1 - xl) * 4 + (z + 2) % 4)
-
-        @pl.loop(5, 8)
-        def _(k):
-            n = arrival(k)
-            dh[...] += dot_nn(Y[n], Wd[n])
-
-        wide_first(*G1, sib_d)
-
-        def slope(r):
-            dpre[r, :] = (dh[r, :] * gelu_slope(pre[r, :])).astype(BF16)
-
-        tiles(rows, 32, slope)
-
-        products("M", dpre, Wu, 0, 3)
+        def backward(i, r):
+            recv(*["Y" + n + i for n in ("bp", "bm")], *["Yd" + "pm"[int(i) - 1] + j for j in "12"])
+            if i == "2":
+                stage_down((1 - xl) * 4 + (z + 2) % 4)
+
+            def more(first, last):
+                @pl.loop(first, last)
+                def _(k):
+                    n = arrival(k)
+                    dh[r] += dot_nn(Y[n, r], Wd[n])
+
+            more(5, 7)
+            if i == "2":
+                wide_first(*G1, sib_d)
+            more(7, 8)
+
+            def slope(t):
+                q = pl.ds(pl.multiple_of(t.start + r.start, 32), t.size)
+                dpre[q, :] = (dh[q, :] * gelu_slope(pre[q, :])).astype(BF16)
+
+            tiles(r.size, 32, slope)
+            if i == "2":
+
+                @pl.loop(0, 2)
+                def _(k):
+                    stage_up(((xl + k) % 2) * 4 + (z + 2) % 4)
+
+            products("M", dpre, Wu, 0, 3, r)
+            if i == "2":
+                wide_third("G", 0, xl, SGD, SIBD, RGD)
+
+        backward("1", H1)
         sent(*["D" + n for n in WAG])
 
         @pl.loop(0, 8)
         def _(b):
             share_d(b).wait_send()
 
-        @pl.loop(0, 2)
-        def _(k):
-            stage_up(((xl + k) % 2) * 4 + (z + 2) % 4)
-
+        backward("2", H2)
         wide_first(*U0, sib_u)
         wide_first(*U1, sib_u)
+        products("M", dpre, Wu, 4, 5)
 
         @pl.loop(0, 3)
         def _(k):
             stage_down((1 - xl) * 4 + (z + 3 + k) % 4)
 
+        rs_first("M", RB)
+        wide_early(*G1, sib_d)
         wide_second(*G1, RGD, sib_d)
-        wide_third("G", 0, xl, SGD, SIBD, RGD)
-        products("M", dpre, Wu, 3, 5)
+        products("M", dpre, Wu, 3, 4)
+        rs_second("M", RB)
+        products("M", dpre, Wu, 5, 8)
 
         @pl.loop(0, 3)
         def _(k):
             stage_up(xl * 4 + (z + 3 + k) % 4)
 
-        rs_first("M", RB)
-        rs_second("M", RB)
+        wide_early(*U0, sib_u)
         wide_second(*U0, RGU, sib_u)
-        products("M", dpre, Wu, 5, 8)
+        rs_third("M", RB)
 
         @pl.loop(0, 3)
         def _(k):
             stage_up((1 - xl) * 4 + (z + 3 + k) % 4)
 
-        rs_third("M", RB)
-        wide_second(*U1, RGU, sib_u)
+        wide_step(*U1, RGU, sib_u)
         wide_third("G", 1, 1 - xl, SGD, SIBD, RGD)
         wide_third("H", 0, xl, SGU, SIBU, RGU)
-        rs_end("M")
+        rs_end("M", 1)
+        rs_end("M", 2)
         for s in range(micro):
 
             def finish(r, s=s):
@@ -612,9 +710,9 @@
 
             tiles(seq, 32, finish)
         back(gt, gt_out, 1).start()
+        wide_third("H", 1, 1 - xl, SGU, SIBU, RGU)
         wide_last("G", xl, SGD, SIBD, RGD, gd)
         back(gd, gd_out, 0).start()
-        wide_third("H", 1, 1 - xl, SGU, SIBU, RGU)
         wide_last("H", xl, SGU, SIBU, RGU, gu)
         back(gu, gu_out, 2).start()
 
@@ -634,7 +732,54 @@
     return kernel
 
 
-TRANSFERS = 18 + 18 + 21 * 2 + 10 * 2 + 17 * 2
+TRANSFERS = 160
+
+
+def widen(*arrays):
+    pieces = 2
+
+    def kernel(*refs):
+        n = len(arrays)
+        src, dst, inner, outer, sems = refs[:n], refs[n : 2 * n], refs[2 * n : 3 * n], refs[3 * n : 4 * n], refs[4 * n]
+
+        def copies(i, j):
+            size = arrays[i].shape[0] // pieces
+            r = pl.ds(j * size, size)
+            return (
+                pltpu.make_async_copy(src[i].at[r], inner[i].at[r], sems.at[0, i, j]),
+                pltpu.make_async_copy(outer[i].at[r], dst[i].at[r], sems.at[1, i, j]),
+                r,
+            )
+
+        every = [copies(i, j) for i in range(n) for j in range(pieces)]
+        for read, _, _ in every:
+            read.start()
+        for k, (read, write, r) in enumerate(every):
+            i = k // pieces
+            read.wait()
+
+            def body(t, i=i, r=r):
+                q = pl.ds(pl.multiple_of(t.start + r.start, 32), t.size)
+                outer[i][q, :] = inner[i][q, :].astype(F32)
+
+            tiles(r.size, 32, body)
+            write.start()
+        for _, write, _ in every:
+            write.wait()
+
+    anys = pl.BlockSpec(memory_space=pl.ANY)
+    return pl.pallas_call(
+        kernel,
+        out_shape=tuple(jax.ShapeDtypeStruct(a.shape, F32) for a in arrays),
+        in_specs=[anys] * len(arrays),
+        out_specs=(anys,) * len(arrays),
+        scratch_shapes=[pltpu.VMEM(a.shape, BF16) for a in arrays]
+        + [pltpu.VMEM(a.shape, F32) for a in arrays]
+        + [pltpu.SemaphoreType.DMA((2, len(arrays), pieces))],
+        compiler_params=pltpu.CompilerParams(vmem_limit_bytes=63 * 2**20),
+        cost_estimate=pl.CostEstimate(flops=0, bytes_accessed=6 * sum(a.size for a in arrays), transcendentals=0),
+        name="widen",
+    )(*arrays)
 
 
 def on_device(tokens, target, mod_table, adv_table, w_up, w_down_t, bins, groups):
@@ -643,8 +788,6 @@
     depth = part * 16
     micro = bins.shape[0]
     scale = float(16 * rows) ** (-0.5)
-    vmem = pl.BlockSpec(memory_space=pltpu.VMEM)
-    smem = pl.BlockSpec(memory_space=pltpu.SMEM)
     anys = pl.BlockSpec(memory_space=pl.ANY)
     block = (8, rows, feat)
     wblock = (8, depth // 8, hidden)
@@ -657,7 +800,7 @@
             jax.ShapeDtypeStruct((part, hidden), BF16),
             jax.ShapeDtypeStruct((part, hidden), BF16),
         ),
-        in_specs=[vmem, anys, vmem, vmem, smem, smem, anys, anys],
+        in_specs=[anys] * 8,
         out_specs=(anys, anys, anys),
         scratch_shapes=[
             V(block, BF16), V(block, BF16), V(wblock, BF16), V(wblock, BF16),
@@ -666,10 +809,12 @@
             V(wblock, BF16), V((8, part, hidden), BF16), V((8, part, hidden), BF16),
             V((7, part, hidden), BF16), V((7, part, hidden), BF16),
             V((8, feat), F32),
+            pltpu.SMEM(bins.shape, jnp.int32), pltpu.SMEM(groups.shape, jnp.int32),
+            V((rows, feat), BF16), V(mod_table.shape, BF16), V(adv_table.shape[::-1], F32),
             V((rows, feat), BF16), V((rows, feat), F32), V((rows, feat), BF16), V((part, hidden), BF16), V((part, hidden), BF16),
             pltpu.SemaphoreType.DMA((TRANSFERS,)),
             pltpu.SemaphoreType.DMA((TRANSFERS,)),
-            pltpu.SemaphoreType.DMA((6,)),
+            pltpu.SemaphoreType.DMA((11,)),
         ],
         compiler_params=pltpu.CompilerParams(
             collective_id=0, has_side_effects=True, vmem_limit_bytes=63 * 2**20
@@ -677,7 +822,7 @@
         cost_estimate=pl.CostEstimate(flops=flops, bytes_accessed=8 * 2**20, transcendentals=2 * rows * hidden),
         name="block_gradient",
     )(tokens, target, mod_table, adv_table.T, bins, groups, w_up, w_down_t)
-    return tuple(g.astype(F32) for g in grads)
+    return widen(*grads)
 
 
 def solution(mesh):

time: 184 us -> 172 us (0.935)
  Pallas kernels: 179 us -> 171 us
  other arithmetic: 4.01 us -> 0 us
    pallas_call x1, Pallas kernels: 179 us -> 169 us  [on_device(): pl.pallas_call(make_kernel(rows, feat, depth, hidden, micro, scale), out_...]
    convert_element_type x3 -> x0, other arithmetic: 4.01 us -> none  [on_device(): return tuple((g.astype(F32) for g in grads))]
    pallas_call x0 -> x1, Pallas kernels: none -> 2.61 us  [widen(): pl.pallas_call(kernel, out_shape=tuple((jax.ShapeDtypeStruct(a.shape, F32...]
where the time goes in v3:
time: 172 us
  Pallas kernels  171 us (99%)
    pallas_call x1, Pallas kernels, on_device(): pl.pallas_call(make_kernel(rows, feat, depth, hidden, micro, scale), out_...  169 us

profile of v3, /device:TPU:2, one launch (start us, length us, event | category | flops | bytes accessed | tf_op | source)
XLA Modules:
  0.0 172.2 jit_solution(9922349907656316520)
XLA Ops:
  0.6 168.8 %block_gradient.1 = (bf16[768,384]{1,0:T(8,128)(2,1)}, bf16[192,896]{1,0:T(8,128)(2,1)}, bf16[192,896]{1,0:T(8,128)(2,1)}) custom-call(bf16[768,384]{1,0:T(8,128)(2,1)} %tok_in.1, bf16[768,384]{1,0:T(8,128)(2,1)} %tgt_in.1, bf16[32,384]{1,0:T(8,128)(2,1)} %mod_in.1, f32[16,32]{1,0:T(8,128)} %bitcast.1, s32[3]{0:T(128)} %bins_in.1, s32[3]{0:T(128)} %grps_in.1, ...), custom_call_target="tpu_custom_call" | custom-call | flops 25367150592 | bytes 8388608 | tf_op jit(solution)/shard_map/block_gradient/pallas_call | solution.py:796
  169.5 2.6 %widen.1 = (f32[768,384]{1,0:T(8,128)}, f32[192,896]{1,0:T(8,128)}, f32[192,896]{1,0:T(8,128)}) custom-call(bf16[768,384]{1,0:T(8,128)(2,1)} %get-tuple-element.6.refs_0_, bf16[192,896]{1,0:T(8,128)(2,1)} %get-tuple-element.7.refs_1_, bf16[192,896]{1,0:T(8,128)(2,1)} %get-tuple-element.8.refs_2_), custom_call_target="tpu_custom_call" | custom-call | bytes 3833856 | tf_op jit(solution)/shard_map/widen/pallas_call | solution.py:771

commit v4 on v3

--- a/solution.py
+++ b/solution.py
@@ -167,7 +167,8 @@
                 one("x" + i, nd(1, 2), r, 0, dnode(1, 0))
                 one("bp" + i, nd(1, 1), r, 2, dnode(0, 1))
                 one("bm" + i, nd(1, -1), r, 3, dnode(0, -1))
-            one("ax", nd(1, 0), W, 4, dnode(1, 0))
+            one("ax1", nd(1, 0), H1, 4, dnode(1, 0))
+            one("ax2", nd(1, 0), H2, 4, dnode(1, 0))
             for i, rp, rm in (("1", K[0], K[2]), ("2", K[1], K[3])):
                 one("cp" + i, nd(0, 2), rp, 1, dnode(0, 1))
                 one("cm" + i, nd(0, 2), rm, 1, dnode(0, -1))
@@ -175,7 +176,7 @@
                 one("ap" + i, nd(0, 1), rp, 5, dnode(0, 1))
                 one("am" + i, nd(0, -1), rm, 6, dnode(0, -1))
 
-        RSN = ["ax"] + [n + i for n in ("x", "bp", "bm", "cp", "cm", "ap", "am") for i in "12"] + ["ap3", "am3"]
+        RSN = [n + i for n in ("x", "ax", "bp", "bm", "cp", "cm", "ap", "am") for i in "12"] + ["ap3", "am3"]
         A1, A2 = pl.ds(0, part // 2), pl.ds(part // 2, part // 2)
         AW = pl.ds(0, part)
 
@@ -216,6 +217,7 @@
         add_rs("M", RB)
         sib_d = add_wrs("G", SGD, RGD, SIBD, xl)
         sib_u = add_wrs("H", SGU, RGU, SIBU, xl)
+        assert count[0] <= TRANSFERS, count[0]
 
         barrier = pltpu.get_barrier_semaphore()
         for dev in (dnode(1, 0), dnode(0, 1), dnode(0, -1), dwide(1, 0), dwide(0, 1), dwide(0, -1), sib):
@@ -289,7 +291,13 @@
         def _():
             start("Dx")
 
-        start("Xx2", "Xx1")
+        start("Xx2")
+
+        @pl.when(same)
+        def _():
+            start("Dx")
+
+        start("Xx1")
 
         def zero(r):
             pre[r, :] = jnp.zeros((r.size, hidden), F32)
@@ -321,11 +329,6 @@
         recv("Xcp1", "Xcp2")
         start("Xdp1", "Xdp2")
         recv("Xcm1", "Xcm2")
-
-        @pl.when(same)
-        def _():
-            start("Dx")
-
         ring_share("U", 1, 1 - xh, share_u)
         ring_end("U", 1, 1 - xh, share_u)
         recv("Xyp3", "Xym3")
@@ -342,26 +345,29 @@
         @pl.loop(0, 5)
         def _(k):
             @pl.when(k == 1)
-            def _():
-                recv("Xx1")
-                start("Xbp1", "Xbm1")
-
-            @pl.when(k == 2)
             def _():
                 recv("Xbp2")
                 start("Xep")
                 recv("Xbm2")
                 start("Xem")
+                recv("Xx1")
+                start("Xbp1", "Xbm1")
+
+            @pl.when(k == 2)
+            def _():
+                ring_relay("D", 0)
 
             n = arrival(k)
             pre[...] += dot_nn(X[n], Wu[n])
 
-        ring_relay("D", 0)
         ring_share("D", 0, 1 - xl, share_d)
 
-        @pl.when(same)
+        @pl.when(~same)
         def _():
-            ring_start("D", 1)
+            recv("Dx")
+            share_d(wm(1, 0)).start()
+
+        ring_start("D", 1)
 
         def forward(i, r):
             if i == "1":
@@ -378,10 +384,10 @@
                 q = pl.ds(pl.multiple_of(t.start + r.start, 32), t.size)
                 hid[q, :] = jax.nn.gelu(pre[q, :], approximate=True).astype(BF16)
 
-            if i == "1":
+            if i == "2":
                 ring_end("D", 0, 1 - xl, share_d)
             tiles(r.size, 32, activate)
-            if i == "1":
+            if i == "2":
                 wait_column(1 - xl, share_d)
             products("P", hid, Wd, 0, 3, r)
 
@@ -422,18 +428,18 @@
 
             tiles(size, 32, body)
 
-        def rs_first(p, R):
-            recv(p + "x1")
-            plus(nd(0, 2), 0, half, R, 0)
-            start(p + "cp1", p + "cp2")
-            recv(p + "x2")
-            plus(nd(0, 2), half, half, R, 0)
-            start(p + "cm1", p + "cm2")
-
-        def rs_second(p, R):
-            recv(*[p + n + i for i in "12" for n in ("bp", "bm")])
-            plus(nd(1, 0), 0, rows, R, 2, 3)
-            start(p + "ax")
+        def rs_first(p, R, order):
+            for i in order:
+                recv(p + "x" + i)
+                plus(nd(0, 2), half * (int(i) - 1), half, R, 0)
+                d = "cp" if i == "1" else "cm"
+                start(p + d + "1", p + d + "2")
+
+        def rs_second(p, R, order):
+            for i in order:
+                recv(p + "bp" + i, p + "bm" + i)
+                plus(nd(1, 0), half * (int(i) - 1), half, R, 2, 3)
+                start(p + "ax" + i)
 
         def rs_third(p, R):
             for i, r in ((1, 0), (2, 1)):
@@ -446,31 +452,25 @@
 
         def rs_end(p, i):
             if i == 1:
-                recv(p + "ax", p + "ap3", p + "am3")
+                recv(p + "ax1", p + "ax2", p + "ap3", p + "am3")
             recv(f"{p}ap{i}", f"{p}am{i}")
 
         def wait_column(b, share):
             for d in range(4):
                 share(b * 4 + d, True).wait_recv()
 
+        forward("2", H2)
+        ring_relay("D", 1)
         forward("1", H1)
-
-        @pl.when(~same)
-        def _():
-            recv("Dx")
-            share_d(wm(1, 0)).start()
-            ring_start("D", 1)
-
-        forward("2", H2)
         products("P", hid, Wd, 3, 4)
-        ring_relay("D", 1)
         ring_share("D", 1, xl, share_d)
         ring_end("D", 1, xl, share_d)
         wait_column(xl, share_d)
         products("P", hid, Wd, 4, 5)
-        rs_first("P", RB)
+        rs_first("P", RB, "2")
         products("P", hid, Wd, 5, 8)
-        rs_second("P", RB)
+        rs_first("P", RB, "1")
+        rs_second("P", RB, "21")
         rs_third("P", RB)
         rs_end("P", 1)
         lt.wait()
@@ -658,9 +658,11 @@
                 def _(k):
                     stage_up(((xl + k) % 2) * 4 + (z + 2) % 4)
 
-            products("M", dpre, Wu, 0, 3, r)
+            products("M", dpre, Wu, 0, 2, r)
             if i == "2":
-                wide_third("G", 0, xl, SGD, SIBD, RGD)
+                wide_first(*U0, sib_u)
+                wide_first(*U1, sib_u)
+            products("M", dpre, Wu, 2, 3, r)
 
         backward("1", H1)
         sent(*["D" + n for n in WAG])
@@ -670,36 +672,36 @@
             share_d(b).wait_send()
 
         backward("2", H2)
-        wide_first(*U0, sib_u)
-        wide_first(*U1, sib_u)
-        products("M", dpre, Wu, 4, 5)
+        wide_third("G", 0, xl, SGD, SIBD, RGD)
+        products("M", dpre, Wu, 3, 5)
+        rs_second("M", RB, "1")
 
         @pl.loop(0, 3)
         def _(k):
             stage_down((1 - xl) * 4 + (z + 3 + k) % 4)
 
-        rs_first("M", RB)
+        rs_first("M", RB, "12")
         wide_early(*G1, sib_d)
         wide_second(*G1, RGD, sib_d)
-        products("M", dpre, Wu, 3, 4)
-        rs_second("M", RB)
-        products("M", dpre, Wu, 5, 8)
 
         @pl.loop(0, 3)
         def _(k):
             stage_up(xl * 4 + (z + 3 + k) % 4)
 
+        rs_second("M", RB, "2")
+        products("M", dpre, Wu, 5, 8)
         wide_early(*U0, sib_u)
         wide_second(*U0, RGU, sib_u)
-        rs_third("M", RB)
 
         @pl.loop(0, 3)
         def _(k):
             stage_up((1 - xl) * 4 + (z + 3 + k) % 4)
 
+        rs_third("M", RB)
         wide_step(*U1, RGU, sib_u)
         wide_third("G", 1, 1 - xl, SGD, SIBD, RGD)
         wide_third("H", 0, xl, SGU, SIBU, RGU)
+        wide_third("H", 1, 1 - xl, SGU, SIBU, RGU)
         rs_end("M", 1)
         rs_end("M", 2)
         for s in range(micro):
@@ -710,7 +712,6 @@
 
             tiles(seq, 32, finish)
         back(gt, gt_out, 1).start()
-        wide_third("H", 1, 1 - xl, SGU, SIBU, RGU)
         wide_last("G", xl, SGD, SIBD, RGD, gd)
         back(gd, gd_out, 0).start()
         wide_last("H", xl, SGU, SIBU, RGU, gu)
@@ -732,7 +733,7 @@
     return kernel
 
 
-TRANSFERS = 160
+TRANSFERS = 176
 
 
 def widen(*arrays):

time: 172 us -> 168 us (0.977)
  Pallas kernels: 171 us -> 167 us
    pallas_call x1, Pallas kernels: 169 us -> 165 us  [on_device(): pl.pallas_call(make_kernel(rows, feat, depth, hidden, micro, scale), out_...]
where the time goes in v4:
time: 168 us
  Pallas kernels  167 us (99%)
    pallas_call x1, Pallas kernels, on_device(): pl.pallas_call(make_kernel(rows, feat, depth, hidden, micro, scale), out_...  165 us

profile of v4, /device:TPU:2, one launch (start us, length us, event | category | flops | bytes accessed | tf_op | source)
XLA Modules:
  0.0 168.2 jit_solution(13964311000433526305)
XLA Ops:
  0.6 164.8 %block_gradient.1 = (bf16[768,384]{1,0:T(8,128)(2,1)}, bf16[192,896]{1,0:T(8,128)(2,1)}, bf16[192,896]{1,0:T(8,128)(2,1)}) custom-call(bf16[768,384]{1,0:T(8,128)(2,1)} %tok_in.1, bf16[768,384]{1,0:T(8,128)(2,1)} %tgt_in.1, bf16[32,384]{1,0:T(8,128)(2,1)} %mod_in.1, f32[16,32]{1,0:T(8,128)} %bitcast.1, s32[3]{0:T(128)} %bins_in.1, s32[3]{0:T(128)} %grps_in.1, ...), custom_call_target="tpu_custom_call" | custom-call | flops 25367150592 | bytes 8388608 | tf_op jit(solution)/shard_map/block_gradient/pallas_call | solution.py:797
  165.4 2.6 %widen.1 = (f32[768,384]{1,0:T(8,128)}, f32[192,896]{1,0:T(8,128)}, f32[192,896]{1,0:T(8,128)}) custom-call(bf16[768,384]{1,0:T(8,128)(2,1)} %get-tuple-element.6.refs_0_, bf16[192,896]{1,0:T(8,128)(2,1)} %get-tuple-element.7.refs_1_, bf16[192,896]{1,0:T(8,128)(2,1)} %get-tuple-element.8.refs_2_), custom_call_target="tpu_custom_call" | custom-call | bytes 3833856 | tf_op jit(solution)/shard_map/widen/pallas_call | solution.py:772

commit v5 on v4

--- a/solution.py
+++ b/solution.py
@@ -41,7 +41,7 @@
         tok_in, tgt_in, mod_in, adv_in, bins_in, grps_in, wu_in, wd_in,
         gt_out, gu_out, gd_out,
         X, Y, Wu, Wd, pre, dh, hid, dpre, SB, RB, SGD, SIBD, SIBU, RGD, RGU, gain,
-        bins, grps, tok, mod, adv, tgt, dpred, gt, gu, gd, ss, rs, ls,
+        bins, grps, tok, mod, adv, tgt, dpred, gt, gu, gd, ss, rs, cs, ls,
     ):
         SGU = Wd
         wi, ni = lax.axis_index("wide"), lax.axis_index("node")
@@ -63,34 +63,56 @@
         sib = (wm(0, 0) * 2 + 1 - c, ni)
 
         table = {}
-        count = [0]
+        slots = {}
+
+        def slot(key):
+            return slots.setdefault(key, len(slots))
 
         def add(name, src, dst, got, dev):
-            table[name] = (count[0], src, dst, got, dev)
-            count[0] += 1
-
-        def desc(name, received):
-            i, src, dst, got, dev = table[name]
-            return pltpu.make_async_remote_copy(
-                src_ref=got if received else src,
-                dst_ref=got if received else dst,
-                send_sem=ss.at[i],
-                recv_sem=rs.at[i],
-                device_id=dev,
-                device_id_type=MESH,
-            )
+            table[name] = (src, dst, got, dev)
 
         def start(*names):
             for name in names:
-                desc(name, False).start()
+                src, dst, _, dev = table[name]
+                pltpu.make_async_remote_copy(
+                    src_ref=src,
+                    dst_ref=dst,
+                    send_sem=ss.at[SENDS.index(name[0])],
+                    recv_sem=rs.at[slot(together(name))],
+                    device_id=dev,
+                    device_id_type=MESH,
+                ).start()
+
+        def bytes_of(ref, send, receive):
+            return pltpu.make_async_remote_copy(
+                src_ref=ref, dst_ref=ref, send_sem=ss.at[send], recv_sem=rs.at[receive], device_id=sib, device_id_type=MESH
+            )
 
         def recv(*names):
+            groups = {}
             for name in names:
-                desc(name, True).wait_recv()
-
-        def sent(*names):
-            for name in names:
-                desc(name, False).wait_send()
+                groups.setdefault(together(name), []).append(name)
+            for key, members in groups.items():
+                assert len(members) == sum(together(name) == key for name in table), key
+                got = table[members[0]][2]
+                if len(members) > 1:
+                    n = sum(table[name][2].shape[0] for name in members)
+                    if members[0][0] in "UDGH":
+                        got = RGD.at[0]
+                        assert n == part
+                    elif n <= rows:
+                        got = RB.at[0, pl.ds(0, n)]
+                    else:
+                        got = RB.at[pl.ds(0, n // half), H1]
+                bytes_of(got, 0, slot(key)).wait_recv()
+
+        def sent(*prefixes):
+            for p in prefixes:
+                bytes_of(RGD if p in "UDGH" else RB, SENDS.index(p), 0).wait_send()
+
+        def shared(*prefixes):
+            for p in prefixes:
+                bytes_of(SIBD, SENDS.index(p.lower()), 0).wait_send()
 
         part = depth // 16
         mine, other = pl.multiple_of(c * part, part), pl.multiple_of((1 - c) * part, part)
@@ -101,6 +123,9 @@
         half = rows // 2
         H1, H2 = pl.ds(0, half), pl.ds(half, half)
         K = [pl.ds(i * (half // 2), half // 2) for i in range(4)]
+        eighth = half // 4
+        T1, T2 = pl.ds(half - eighth, eighth), pl.ds(rows - eighth, eighth)
+        L1, L2 = pl.ds(0, half - eighth), pl.ds(half, half - eighth)
 
         def add_ag(p, B, fewer):
             def one(name, blk, r, got, dev):
@@ -111,8 +136,12 @@
                 one("ym" + i, nd(0, 0), rm, nd(0, 1), dnode(0, -1))
             for i, r in (("1", H1), ("2", H2)):
                 one("x" + i, nd(0, 0), r, nd(1, 0), dnode(1, 0))
-                one("bp" + i, nd(1, 0), r, nd(1, -1), dnode(0, 1))
-                one("bm" + i, nd(1, 0), r, nd(1, 1), dnode(0, -1))
+                b = L2 if i == "2" and not fewer else r
+                one("bp" + i, nd(1, 0), b, nd(1, -1), dnode(0, 1))
+                one("bm" + i, nd(1, 0), b, nd(1, 1), dnode(0, -1))
+            if not fewer:
+                one("tp", nd(0, -1), T2, nd(1, -1), dnode(1, 0))
+                one("tm", nd(0, 1), T2, nd(1, 1), dnode(1, 0))
             for i, rp, rm in (("1", K[0], K[2]), ("2", K[1], K[3])):
                 one("cp" + i, nd(0, -1), rp, nd(0, 2), dnode(0, 1))
                 one("cm" + i, nd(0, 1), rm, nd(0, 2), dnode(0, -1))
@@ -123,11 +152,6 @@
                 one("ep", nd(1, -1), K[2], nd(1, 2), dnode(0, 1))
                 one("em", nd(1, 1), K[3], nd(1, 2), dnode(0, -1))
 
-        def ag_names(p, fewer):
-            names = ["yp", "ym", "x", "bp", "bm", "cp", "cm", "dp"] + ([] if fewer else ["dm"])
-            last = ["yp3", "ym3"] + (["ep", "em"] if fewer else [])
-            return [p + n + i for n in names for i in "12"] + [p + n for n in last]
-
         def add_wag(p, B, b0):
             def one(name, blk, r, got, dev):
                 add(p + name, B.at[blk, r], B.at[blk, r], B.at[got, r], dev)
@@ -141,23 +165,29 @@
                 one(f"ym{i}", here, Q1, up, dwide(0, -1))
                 one(f"cp{i}", down, Q1, far, dwide(0, 1))
                 one(f"cm{i}", up, Q2, far, dwide(0, -1))
-            base = count[0]
-            count[0] += 8
-
-            def share(b, received=False):
-                r = PS if received else PC
+            def share(b):
+                column = jnp.where(b // 4 == b0, 0, 1)
                 return pltpu.make_async_remote_copy(
-                    src_ref=B.at[b, r],
-                    dst_ref=B.at[b, r],
-                    send_sem=ss.at[base + b],
-                    recv_sem=rs.at[base + b],
+                    src_ref=B.at[b, PC],
+                    dst_ref=B.at[b, PC],
+                    send_sem=ss.at[SENDS.index(p.lower())],
+                    recv_sem=cs.at[(0 if p == "U" else 2) + column],
                     device_id=sib,
                     device_id_type=MESH,
                 )
 
-            return share
-
-        WAG = ("x",) + tuple(f"{n}{i}" for i in (0, 1) for n in ("zp", "zm", "yp", "ym", "cp", "cm"))
+            def column_shared(i):
+                ref = SIBD.at[pl.ds(0, 4)]
+                pltpu.make_async_remote_copy(
+                    src_ref=ref,
+                    dst_ref=ref,
+                    send_sem=ss.at[0],
+                    recv_sem=cs.at[(0 if p == "U" else 2) + i],
+                    device_id=sib,
+                    device_id_type=MESH,
+                ).wait_recv()
+
+            return share, column_shared
 
         def add_rs(p, R):
             def one(name, blk, r, slot, dev):
@@ -165,8 +195,11 @@
 
             for i, r in (("1", H1), ("2", H2)):
                 one("x" + i, nd(1, 2), r, 0, dnode(1, 0))
-                one("bp" + i, nd(1, 1), r, 2, dnode(0, 1))
-                one("bm" + i, nd(1, -1), r, 3, dnode(0, -1))
+                one("bp" + i, nd(1, 1), L1 if i == "1" and p == "P" else r, 2, dnode(0, 1))
+                one("bm" + i, nd(1, -1), L2 if i == "2" and p == "P" else r, 3, dnode(0, -1))
+            if p == "P":
+                one("tp", nd(1, 1), T1, 2, dnode(1, 0))
+                one("tm", nd(1, -1), T2, 3, dnode(1, 0))
             one("ax1", nd(1, 0), H1, 4, dnode(1, 0))
             one("ax2", nd(1, 0), H2, 4, dnode(1, 0))
             for i, rp, rm in (("1", K[0], K[2]), ("2", K[1], K[3])):
@@ -176,7 +209,6 @@
                 one("ap" + i, nd(0, 1), rp, 5, dnode(0, 1))
                 one("am" + i, nd(0, -1), rm, 6, dnode(0, -1))
 
-        RSN = [n + i for n in ("x", "ax", "bp", "bm", "cp", "cm", "ap", "am") for i in "12"] + ["ap3", "am3"]
         A1, A2 = pl.ds(0, part // 2), pl.ds(part // 2, part // 2)
         AW = pl.ds(0, part)
 
@@ -193,31 +225,28 @@
                 for h, r, a in (("a", Q1, A1), ("b", Q2, A2)):
                     one(f"ap{i}{h}", up, r, 2 + 2 * i, a, dwide(0, 1))
                     one(f"am{i}{h}", down, r, 3 + 2 * i, a, dwide(0, -1))
-            base = count[0]
-            count[0] += 8
+            base = 4 if p == "G" else 12
 
             def share(b):
                 return pltpu.make_async_remote_copy(
                     src_ref=S.at[b, PS],
                     dst_ref=B.at[b],
-                    send_sem=ss.at[base + b],
-                    recv_sem=rs.at[base + b],
+                    send_sem=ss.at[SENDS.index(p.lower())],
+                    recv_sem=cs.at[base + b],
                     device_id=sib,
                     device_id_type=MESH,
                 )
 
             return share
 
-        RSW = ("xa", "xb") + tuple(n.format(i) for i in (0, 1) for n in ("cp{}", "cm{}", "ap{}a", "ap{}b", "am{}a", "am{}b"))
         add_ag("X", X, True)
         add_ag("Y", Y, False)
-        share_u = add_wag("U", Wu, xh)
-        share_d = add_wag("D", Wd, 1 - xl)
+        share_u, column_u = add_wag("U", Wu, xh)
+        share_d, column_d = add_wag("D", Wd, 1 - xl)
         add_rs("P", RB)
         add_rs("M", RB)
         sib_d = add_wrs("G", SGD, RGD, SIBD, xl)
         sib_u = add_wrs("H", SGU, RGU, SIBU, xl)
-        assert count[0] <= TRANSFERS, count[0]
 
         barrier = pltpu.get_barrier_semaphore()
         for dev in (dnode(1, 0), dnode(0, 1), dnode(0, -1), dwide(1, 0), dwide(0, 1), dwide(0, -1), sib):
@@ -333,9 +362,8 @@
         ring_end("U", 1, 1 - xh, share_u)
         recv("Xyp3", "Xym3")
 
-        @pl.loop(0, 8)
-        def _(b):
-            share_u(b, True).wait_recv()
+        column_u(0)
+        column_u(1)
 
         def arrival(k):
             dx = jnp.where((k == 3) | (k >= 5), 1, 0)
@@ -388,7 +416,7 @@
                 ring_end("D", 0, 1 - xl, share_d)
             tiles(r.size, 32, activate)
             if i == "2":
-                wait_column(1 - xl, share_d)
+                column_d(0)
             products("P", hid, Wd, 0, 3, r)
 
         def departure(k):
@@ -408,6 +436,8 @@
                         def _(name=name):
                             if r.start == 0:
                                 start(p + name + "1")
+                                if p == "P" and name != "x":
+                                    start(p + "t" + name[1])
                             if r.start + r.size == rows:
                                 start(p + name + "2")
 
@@ -438,26 +468,33 @@
         def rs_second(p, R, order):
             for i in order:
                 recv(p + "bp" + i, p + "bm" + i)
-                plus(nd(1, 0), half * (int(i) - 1), half, R, 2, 3)
+                if p == "P":
+                    low, last = (L1, T1) if i == "1" else (L2, T2)
+                    plus(nd(1, 0), low.start, low.size, R, 2, 3)
+                    plus(nd(1, 0), last.start, last.size, R, 3 if i == "1" else 2)
+                else:
+                    plus(nd(1, 0), half * (int(i) - 1), half, R, 2, 3)
                 start(p + "ax" + i)
 
         def rs_third(p, R):
             for i, r in ((1, 0), (2, 1)):
                 recv(f"{p}cp{i}")
                 plus(nd(0, 1), K[r].start, half // 2, R, 1)
+                if p == "P" and i == 2:
+                    recv("Ptp")
+                    plus(nd(0, 1), T1.start, eighth, R, 2)
                 start(f"{p}ap{i}")
                 recv(f"{p}cm{i}")
                 plus(nd(0, -1), K[r + 2].start, half // 2, R, 1)
+                if p == "P" and i == 2:
+                    recv("Ptm")
+                    plus(nd(0, -1), T2.start, eighth, R, 3)
                 start(f"{p}am{i}")
 
         def rs_end(p, i):
             if i == 1:
                 recv(p + "ax1", p + "ax2", p + "ap3", p + "am3")
             recv(f"{p}ap{i}", f"{p}am{i}")
-
-        def wait_column(b, share):
-            for d in range(4):
-                share(b * 4 + d, True).wait_recv()
 
         forward("2", H2)
         ring_relay("D", 1)
@@ -465,7 +502,7 @@
         products("P", hid, Wd, 3, 4)
         ring_share("D", 1, xl, share_d)
         ring_end("D", 1, xl, share_d)
-        wait_column(xl, share_d)
+        column_d(1)
         products("P", hid, Wd, 4, 5)
         rs_first("P", RB, "2")
         products("P", hid, Wd, 5, 8)
@@ -508,7 +545,7 @@
         error(1)
         error(3)
         start("Yyp2", "Yym2", "Yx1", "Yx2", "Yyp3", "Yym3")
-        sent(*["P" + n for n in RSN])
+        sent("P")
 
         def stage_down(m):
             SGD[m] = (dot_tn(Y[m], hid[...]) * scale).astype(BF16)
@@ -609,6 +646,7 @@
                 recv("Yx2")
                 start("Ybp2", "Ybm2")
                 recv("Yyp3", "Yym3")
+                start("Ytp", "Ytm")
 
             @pl.when(k == 4)
             def _():
@@ -632,7 +670,8 @@
         dh[...] += dot_nn(Y[last], Wd[last])
         wide_second(*G0, RGD, sib_d)
         def backward(i, r):
-            recv(*["Y" + n + i for n in ("bp", "bm")], *["Yd" + "pm"[int(i) - 1] + j for j in "12"])
+            late = ["Ytp", "Ytm"] if i == "2" else []
+            recv(*["Y" + n + i for n in ("bp", "bm")], *["Yd" + "pm"[int(i) - 1] + j for j in "12"], *late)
             if i == "2":
                 stage_down((1 - xl) * 4 + (z + 2) % 4)
 
@@ -665,11 +704,8 @@
             products("M", dpre, Wu, 2, 3, r)
 
         backward("1", H1)
-        sent(*["D" + n for n in WAG])
-
-        @pl.loop(0, 8)
-        def _(b):
-            share_d(b).wait_send()
+        sent("D")
+        shared("D")
 
         backward("2", H2)
         wide_third("G", 0, xl, SGD, SIBD, RGD)
@@ -717,15 +753,9 @@
         wide_last("H", xl, SGU, SIBU, RGU, gu)
         back(gu, gu_out, 2).start()
 
-        sent(*ag_names("X", True), *ag_names("Y", False), *["U" + n for n in WAG], *["M" + n for n in RSN])
-        sent(*["G" + n for n in RSW], *["H" + n for n in RSW])
-
-        @pl.loop(0, 8)
-        def _(b):
-            share_u(b).wait_send()
-            sib_d(b).wait_send()
-            sib_u(b).wait_send()
-
+        sent("X", "Y", "U", "M", "G", "H")
+        shared("U", "G", "H")
+        assert len(slots) == RECEIVES, len(slots)
         back(gd, gd_out, 0).wait()
         back(gt, gt_out, 1).wait()
         back(gu, gu_out, 2).wait()
@@ -733,7 +763,35 @@
     return kernel
 
 
-TRANSFERS = 176
+SENDS = "XYUDPMGHudgh"
+
+
+def together(name):
+    p, n = name[0], name[1:]
+    if n in ("yp3", "ym3"):
+        return p + "y3"
+    if p in "XY" and n in ("bp1", "bm1", "dp1", "dp2"):
+        return p + "n1"
+    if (p == "Y" and n in ("bp2", "bm2", "dm1", "dm2", "tp", "tm")) or (p == "X" and n in ("ep", "em")):
+        return p + "n2"
+    if p == "X" and n in ("cm1", "cm2"):
+        return "Xcm"
+    if p in "PM":
+        if n in ("ax1", "ax2", "ap3", "am3"):
+            return p + "n"
+        if n[:2] in ("bp", "bm"):
+            return p + "b" + n[2]
+    if p in "UD" and n[:2] in ("cp", "cm"):
+        return p + "c" + n[2]
+    if p in "GH":
+        if n[0] == "x":
+            return p + "x"
+        if n[0] == "a":
+            return p + "a" + n[2:]
+    return name
+
+
+RECEIVES = 95
 
 
 def widen(*arrays):
@@ -813,8 +871,9 @@
             pltpu.SMEM(bins.shape, jnp.int32), pltpu.SMEM(groups.shape, jnp.int32),
             V((rows, feat), BF16), V(mod_table.shape, BF16), V(adv_table.shape[::-1], F32),
             V((rows, feat), BF16), V((rows, feat), F32), V((rows, feat), BF16), V((part, hidden), BF16), V((part, hidden), BF16),
-            pltpu.SemaphoreType.DMA((TRANSFERS,)),
-            pltpu.SemaphoreType.DMA((TRANSFERS,)),
+            pltpu.SemaphoreType.DMA((len(SENDS),)),
+            pltpu.SemaphoreType.DMA((RECEIVES,)),
+            pltpu.SemaphoreType.DMA((20,)),
             pltpu.SemaphoreType.DMA((11,)),
         ],
         compiler_params=pltpu.CompilerParams(

time: 168 us -> 164 us (0.976)
  Pallas kernels: 167 us -> 163 us
    pallas_call x1, Pallas kernels: 165 us -> 160 us  [on_device(): pl.pallas_call(make_kernel(rows, feat, depth, hidden, micro, scale), out_...]
where the time goes in v5:
time: 164 us
  Pallas kernels  163 us (99%)
    pallas_call x1, Pallas kernels, on_device(): pl.pallas_call(make_kernel(rows, feat, depth, hidden, micro, scale), out_...  160 us

profile of v5, /device:TPU:2, one launch (start us, length us, event | category | flops | bytes accessed | tf_op | source)
XLA Modules:
  0.0 163.7 jit_solution(7765313763914657736)
XLA Ops:
  0.6 160.3 %block_gradient.1 = (bf16[768,384]{1,0:T(8,128)(2,1)}, bf16[192,896]{1,0:T(8,128)(2,1)}, bf16[192,896]{1,0:T(8,128)(2,1)}) custom-call(bf16[768,384]{1,0:T(8,128)(2,1)} %tok_in.1, bf16[768,384]{1,0:T(8,128)(2,1)} %tgt_in.1, bf16[32,384]{1,0:T(8,128)(2,1)} %mod_in.1, f32[16,32]{1,0:T(8,128)} %bitcast.1, s32[3]{0:T(128)} %bins_in.1, s32[3]{0:T(128)} %grps_in.1, ...), custom_call_target="tpu_custom_call" | custom-call | flops 25367150592 | bytes 8388608 | tf_op jit(solution)/shard_map/block_gradient/pallas_call | solution.py:855
  161.0 2.6 %widen.1 = (f32[768,384]{1,0:T(8,128)}, f32[192,896]{1,0:T(8,128)}, f32[192,896]{1,0:T(8,128)}) custom-call(bf16[768,384]{1,0:T(8,128)(2,1)} %get-tuple-element.6.refs_0_, bf16[192,896]{1,0:T(8,128)(2,1)} %get-tuple-element.7.refs_1_, bf16[192,896]{1,0:T(8,128)(2,1)} %get-tuple-element.8.refs_2_), custom_call_target="tpu_custom_call" | custom-call | bytes 3833856 | tf_op jit(solution)/shard_map/widen/pallas_call | solution.py:830

commit v6 on v5

--- a/solution.py
+++ b/solution.py
@@ -135,11 +135,14 @@
                 one("yp" + i, nd(0, 0), rp, nd(0, -1), dnode(0, 1))
                 one("ym" + i, nd(0, 0), rm, nd(0, 1), dnode(0, -1))
             for i, r in (("1", H1), ("2", H2)):
-                one("x" + i, nd(0, 0), r, nd(1, 0), dnode(1, 0))
+                if fewer:
+                    one("x" + i, nd(0, 0), r, nd(1, 0), dnode(1, 0))
                 b = L2 if i == "2" and not fewer else r
                 one("bp" + i, nd(1, 0), b, nd(1, -1), dnode(0, 1))
                 one("bm" + i, nd(1, 0), b, nd(1, 1), dnode(0, -1))
             if not fewer:
+                for i, r in (("1", K[0]), ("2", K[2]), ("3", K[1]), ("4", K[3])):
+                    one("x" + i, nd(0, 0), r, nd(1, 0), dnode(1, 0))
                 one("tp", nd(0, -1), T2, nd(1, -1), dnode(1, 0))
                 one("tm", nd(0, 1), T2, nd(1, 1), dnode(1, 0))
             for i, rp, rm in (("1", K[0], K[2]), ("2", K[1], K[3])):
@@ -540,11 +543,11 @@
 
         error(0)
         error(2)
-        start("Yyp1", "Yym1")
+        start("Yyp1", "Yym1", "Yx1", "Yx2")
         rs_end("P", 2)
         error(1)
         error(3)
-        start("Yyp2", "Yym2", "Yx1", "Yx2", "Yyp3", "Yym3")
+        start("Yyp2", "Yym2", "Yx3", "Yx4", "Yyp3", "Yym3")
         sent("P")
 
         def stage_down(m):
@@ -641,18 +644,20 @@
             @pl.when(k == 1)
             def _():
                 far_relay("Y")
-                recv("Yx1")
+                recv("Yx1", "Yx2", "Yx3")
                 start("Ybp1", "Ybm1")
-                recv("Yx2")
+                recv("Yx4")
                 start("Ybp2", "Ybm2")
                 recv("Yyp3", "Yym3")
                 start("Ytp", "Ytm")
 
-            @pl.when(k == 4)
-            def _():
-                for d in ("p1", "p2", "m1", "m2"):
-                    recv("Yc" + d)
-                    start("Yd" + d)
+            for at, ds in ((2, ("p1",)), (3, ("p2", "m1", "m2"))):
+
+                @pl.when(k == at)
+                def _(ds=ds):
+                    for d in ds:
+                        recv("Yc" + d)
+                        start("Yd" + d)
 
             n = arrival(k)
 
@@ -668,7 +673,6 @@
         wide_early(*G0, sib_d)
         last = arrival(4)
         dh[...] += dot_nn(Y[last], Wd[last])
-        wide_second(*G0, RGD, sib_d)
         def backward(i, r):
             late = ["Ytp", "Ytm"] if i == "2" else []
             recv(*["Y" + n + i for n in ("bp", "bm")], *["Yd" + "pm"[int(i) - 1] + j for j in "12"], *late)
@@ -697,27 +701,30 @@
                 def _(k):
                     stage_up(((xl + k) % 2) * 4 + (z + 2) % 4)
 
-            products("M", dpre, Wu, 0, 2, r)
             if i == "2":
                 wide_first(*U0, sib_u)
+                products("M", dpre, Wu, 0, 1, r)
                 wide_first(*U1, sib_u)
-            products("M", dpre, Wu, 2, 3, r)
+                products("M", dpre, Wu, 1, 3, r)
+            else:
+                products("M", dpre, Wu, 0, 3, r)
 
         backward("1", H1)
+        wide_second(*G0, RGD, sib_d)
         sent("D")
         shared("D")
 
         backward("2", H2)
         wide_third("G", 0, xl, SGD, SIBD, RGD)
-        products("M", dpre, Wu, 3, 5)
-        rs_second("M", RB, "1")
 
         @pl.loop(0, 3)
         def _(k):
             stage_down((1 - xl) * 4 + (z + 3 + k) % 4)
 
+        products("M", dpre, Wu, 3, 5)
+        wide_early(*G1, sib_d)
+        rs_second("M", RB, "1")
         rs_first("M", RB, "12")
-        wide_early(*G1, sib_d)
         wide_second(*G1, RGD, sib_d)
 
         @pl.loop(0, 3)
@@ -791,11 +798,11 @@
     return name
 
 
-RECEIVES = 95
+RECEIVES = 97
 
 
 def widen(*arrays):
-    pieces = 2
+    pieces = 3
 
     def kernel(*refs):
         n = len(arrays)

time: 164 us -> 161 us (0.982)
  Pallas kernels: 163 us -> 159 us
    pallas_call x1, Pallas kernels: 160 us -> 157 us  [on_device(): pl.pallas_call(make_kernel(rows, feat, depth, hidden, micro, scale), out_...]
where the time goes in v6:
time: 161 us; the launch traced here: 160 us
  Pallas kernels  159 us (99%)
    pallas_call x1, Pallas kernels, on_device(): pl.pallas_call(make_kernel(rows, feat, depth, hidden, micro, scale), out_...  157 us

profile of v6, /device:TPU:2, one launch (start us, length us, event | category | flops | bytes accessed | tf_op | source)
XLA Modules:
  0.0 160.2 jit_solution(15134335079137958728)
XLA Ops:
  0.6 156.8 %block_gradient.1 = (bf16[768,384]{1,0:T(8,128)(2,1)}, bf16[192,896]{1,0:T(8,128)(2,1)}, bf16[192,896]{1,0:T(8,128)(2,1)}) custom-call(bf16[768,384]{1,0:T(8,128)(2,1)} %tok_in.1, bf16[768,384]{1,0:T(8,128)(2,1)} %tgt_in.1, bf16[32,384]{1,0:T(8,128)(2,1)} %mod_in.1, f32[16,32]{1,0:T(8,128)} %bitcast.1, s32[3]{0:T(128)} %bins_in.1, s32[3]{0:T(128)} %grps_in.1, ...), custom_call_target="tpu_custom_call" | custom-call | flops 25367150592 | bytes 8388608 | tf_op jit(solution)/shard_map/block_gradient/pallas_call | solution.py:862
  157.4 2.6 %widen.1 = (f32[768,384]{1,0:T(8,128)}, f32[192,896]{1,0:T(8,128)}, f32[192,896]{1,0:T(8,128)}) custom-call(bf16[768,384]{1,0:T(8,128)(2,1)} %get-tuple-element.6.refs_0_, bf16[192,896]{1,0:T(8,128)(2,1)} %get-tuple-element.7.refs_1_, bf16[192,896]{1,0:T(8,128)(2,1)} %get-tuple-element.8.refs_2_), custom_call_target="tpu_custom_call" | custom-call | bytes 3833856 | tf_op jit(solution)/shard_map/widen/pallas_call | solution.py:837

commit v7 on v6

--- a/solution.py
+++ b/solution.py
@@ -197,9 +197,15 @@
                 add(p + name, SB.at[blk, r], R.at[slot, r], R.at[slot, r], dev)
 
             for i, r in (("1", H1), ("2", H2)):
-                one("x" + i, nd(1, 2), r, 0, dnode(1, 0))
-                one("bp" + i, nd(1, 1), L1 if i == "1" and p == "P" else r, 2, dnode(0, 1))
-                one("bm" + i, nd(1, -1), L2 if i == "2" and p == "P" else r, 3, dnode(0, -1))
+                low = L1 if i == "1" else L2
+                one("x" + i, nd(1, 2), low if p == "M" else r, 0, dnode(1, 0))
+                one("bp" + i, nd(1, 1), low if i == "1" else r, 2, dnode(0, 1))
+                one("bm" + i, nd(1, -1), low if i == "2" else r, 3, dnode(0, -1))
+            if p == "M":
+                one("ep", nd(1, 2), T1, 0, dnode(0, 1))
+                one("em", nd(1, 2), T2, 0, dnode(0, -1))
+                one("fp", nd(1, 1), T1, 2, dnode(0, 1))
+                one("fm", nd(1, -1), T2, 3, dnode(0, -1))
             if p == "P":
                 one("tp", nd(1, 1), T1, 2, dnode(1, 0))
                 one("tm", nd(1, -1), T2, 3, dnode(1, 0))
@@ -381,12 +387,9 @@
                 start("Xep")
                 recv("Xbm2")
                 start("Xem")
+                ring_relay("D", 0)
                 recv("Xx1")
                 start("Xbp1", "Xbm1")
-
-            @pl.when(k == 2)
-            def _():
-                ring_relay("D", 0)
 
             n = arrival(k)
             pre[...] += dot_nn(X[n], Wu[n])
@@ -441,8 +444,12 @@
                                 start(p + name + "1")
                                 if p == "P" and name != "x":
                                     start(p + "t" + name[1])
+                                if p == "M" and name == "x":
+                                    start("Mep")
                             if r.start + r.size == rows:
                                 start(p + name + "2")
+                                if p == "M" and name == "x":
+                                    start("Mem")
 
                 for at, name in ((5, "ap3"), (6, "am3")):
                     if first <= at < last:
@@ -464,13 +471,13 @@
         def rs_first(p, R, order):
             for i in order:
                 recv(p + "x" + i)
-                plus(nd(0, 2), half * (int(i) - 1), half, R, 0)
+                plus(nd(0, 2), half * (int(i) - 1), half if p == "P" else half - eighth, R, 0)
                 d = "cp" if i == "1" else "cm"
                 start(p + d + "1", p + d + "2")
 
         def rs_second(p, R, order):
             for i in order:
-                recv(p + "bp" + i, p + "bm" + i)
+                recv(p + "bp" + i, p + "bm" + i, *(["Mfp" if i == "1" else "Mfm"] if p == "M" else []))
                 if p == "P":
                     low, last = (L1, T1) if i == "1" else (L2, T2)
                     plus(nd(1, 0), low.start, low.size, R, 2, 3)
@@ -478,6 +485,12 @@
                 else:
                     plus(nd(1, 0), half * (int(i) - 1), half, R, 2, 3)
                 start(p + "ax" + i)
+
+        def pass_on(i):
+            recv("Mep" if i == "1" else "Mem")
+            blk, r = (nd(1, 1), T1) if i == "1" else (nd(1, -1), T2)
+            plus(blk, r.start, r.size, RB, 0)
+            start("Mfp" if i == "1" else "Mfm")
 
         def rs_third(p, R):
             for i, r in ((1, 0), (2, 1)):
@@ -665,14 +678,18 @@
             def _():
                 stage_down(n)
 
-            @pl.when(k != 4)
+            @pl.when(k < 3)
             def _():
                 dh[...] += dot_nn(Y[n], Wd[n])
 
         wide_first(*G0, sib_d)
         wide_early(*G0, sib_d)
-        last = arrival(4)
-        dh[...] += dot_nn(Y[last], Wd[last])
+
+        @pl.loop(3, 5)
+        def _(k):
+            n = arrival(k)
+            dh[...] += dot_nn(Y[n], Wd[n])
+
         def backward(i, r):
             late = ["Ytp", "Ytm"] if i == "2" else []
             recv(*["Y" + n + i for n in ("bp", "bm")], *["Yd" + "pm"[int(i) - 1] + j for j in "12"], *late)
@@ -685,10 +702,10 @@
                     n = arrival(k)
                     dh[r] += dot_nn(Y[n, r], Wd[n])
 
-            more(5, 7)
+            more(5, 6)
             if i == "2":
                 wide_first(*G1, sib_d)
-            more(7, 8)
+            more(6, 8)
 
             def slope(t):
                 q = pl.ds(pl.multiple_of(t.start + r.start, 32), t.size)
@@ -703,14 +720,16 @@
 
             if i == "2":
                 wide_first(*U0, sib_u)
+                pass_on("1")
                 products("M", dpre, Wu, 0, 1, r)
                 wide_first(*U1, sib_u)
                 products("M", dpre, Wu, 1, 3, r)
             else:
-                products("M", dpre, Wu, 0, 3, r)
+                products("M", dpre, Wu, 0, 1, r)
+                wide_second(*G0, RGD, sib_d)
+                products("M", dpre, Wu, 1, 3, r)
 
         backward("1", H1)
-        wide_second(*G0, RGD, sib_d)
         sent("D")
         shared("D")
 
@@ -721,6 +740,7 @@
         def _(k):
             stage_down((1 - xl) * 4 + (z + 3 + k) % 4)
 
+        pass_on("2")
         products("M", dpre, Wu, 3, 5)
         wide_early(*G1, sib_d)
         rs_second("M", RB, "1")
@@ -788,6 +808,8 @@
             return p + "n"
         if n[:2] in ("bp", "bm"):
             return p + "b" + n[2]
+        if n in ("fp", "fm"):
+            return p + ("b1" if n == "fp" else "b2")
     if p in "UD" and n[:2] in ("cp", "cm"):
         return p + "c" + n[2]
     if p in "GH":
@@ -798,7 +820,7 @@
     return name
 
 
-RECEIVES = 97
+RECEIVES = 99
 
 
 def widen(*arrays):

time: 161 us -> 160 us (level)
  no operation moved by 1% of the time
where the time goes in v7:
time: 160 us
  Pallas kernels  159 us (99%)
    pallas_call x1, Pallas kernels, on_device(): pl.pallas_call(make_kernel(rows, feat, depth, hidden, micro, scale), out_...  157 us

profile of v7, /device:TPU:2, one launch (start us, length us, event | category | flops | bytes accessed | tf_op | source)
XLA Modules:
  0.0 159.9 jit_solution(11153748673426425026)
XLA Ops:
  0.6 156.5 %block_gradient.1 = (bf16[768,384]{1,0:T(8,128)(2,1)}, bf16[192,896]{1,0:T(8,128)(2,1)}, bf16[192,896]{1,0:T(8,128)(2,1)}) custom-call(bf16[768,384]{1,0:T(8,128)(2,1)} %tok_in.1, bf16[768,384]{1,0:T(8,128)(2,1)} %tgt_in.1, bf16[32,384]{1,0:T(8,128)(2,1)} %mod_in.1, f32[16,32]{1,0:T(8,128)} %bitcast.1, s32[3]{0:T(128)} %bins_in.1, s32[3]{0:T(128)} %grps_in.1, ...), custom_call_target="tpu_custom_call" | custom-call | flops 25367150592 | bytes 8388608 | tf_op jit(solution)/shard_map/block_gradient/pallas_call | solution.py:884
  157.2 2.6 %widen.1 = (f32[768,384]{1,0:T(8,128)}, f32[192,896]{1,0:T(8,128)}, f32[192,896]{1,0:T(8,128)}) custom-call(bf16[768,384]{1,0:T(8,128)(2,1)} %get-tuple-element.6.refs_0_, bf16[192,896]{1,0:T(8,128)(2,1)} %get-tuple-element.7.refs_1_, bf16[192,896]{1,0:T(8,128)(2,1)} %get-tuple-element.8.refs_2_), custom_call_target="tpu_custom_call" | custom-call | bytes 3833856 | tf_op jit(solution)/shard_map/widen/pallas_call | solution.py:859

commit v8 on v7

--- a/solution.py
+++ b/solution.py
@@ -634,19 +634,26 @@
                     wide_plus(S, m, ((B, m), (R, 2 + 2 * i), (R, 3 + 2 * i)), r0, quarter)
                     start(p + "x" + h)
 
-        def wide_last(p, b0, S, B, R, out):
-            recv(p + "xa", p + "xb")
+        def wide_last(p, b0, S, B, R, out, leave):
             m = wm(0, 0)
-            slot = jnp.where(xh == b0, 2, 4)
-
-            def body(r):
-                q = pl.ds(pl.multiple_of(mine + r.start, 32), r.size)
-                v = S[m, q, :].astype(F32) + B[m, r, :].astype(F32)
-                v = v + R[slot, r, :].astype(F32) + R[slot + 1, r, :].astype(F32)
-                out[r, :] = (v + R[6, r, :].astype(F32)).astype(BF16)
-
-            tiles(part, 32, body)
-
+            first = jnp.where(xh == b0, 2, 4)
+            for h, r0 in (("a", 0), ("b", quarter)):
+                recv(p + "x" + h)
+
+                def body(r, r0=r0):
+                    a = pl.ds(pl.multiple_of(r.start + r0, 32), r.size)
+                    q = pl.ds(pl.multiple_of(mine + r.start + r0, 32), r.size)
+                    v = S[m, q, :].astype(F32) + B[m, a, :].astype(F32)
+                    v = v + R[first, a, :].astype(F32) + R[first + 1, a, :].astype(F32)
+                    out[a, :] = (v + R[6, a, :].astype(F32)).astype(BF16)
+
+                tiles(quarter, 32, body)
+                leave[h].start()
+
+        def leaving(src, dst, i):
+            return {h: back(src.at[r], dst.at[r], i + (h == "b")) for h, r in (("a", A1), ("b", A2))}
+
+        leave_d, leave_u = leaving(gd, gd_out, 8), leaving(gu, gu_out, 10)
         G0 = ("G", 0, xl, SGD, SIBD)
         G1 = ("G", 1, 1 - xl, SGD, SIBD)
         U0 = ("H", 0, xl, SGU, SIBU)
@@ -775,17 +782,16 @@
 
             tiles(seq, 32, finish)
         back(gt, gt_out, 1).start()
-        wide_last("G", xl, SGD, SIBD, RGD, gd)
-        back(gd, gd_out, 0).start()
-        wide_last("H", xl, SGU, SIBU, RGU, gu)
-        back(gu, gu_out, 2).start()
+        wide_last("G", xl, SGD, SIBD, RGD, gd, leave_d)
+        wide_last("H", xl, SGU, SIBU, RGU, gu, leave_u)
 
         sent("X", "Y", "U", "M", "G", "H")
         shared("U", "G", "H")
         assert len(slots) == RECEIVES, len(slots)
-        back(gd, gd_out, 0).wait()
         back(gt, gt_out, 1).wait()
-        back(gu, gu_out, 2).wait()
+        for h in "ab":
+            leave_d[h].wait()
+            leave_u[h].wait()
 
     return kernel
 
@@ -813,14 +819,12 @@
     if p in "UD" and n[:2] in ("cp", "cm"):
         return p + "c" + n[2]
     if p in "GH":
-        if n[0] == "x":
-            return p + "x"
         if n[0] == "a":
             return p + "a" + n[2:]
     return name
 
 
-RECEIVES = 99
+RECEIVES = 101
 
 
 def widen(*arrays):
@@ -903,7 +907,7 @@
             pltpu.SemaphoreType.DMA((len(SENDS),)),
             pltpu.SemaphoreType.DMA((RECEIVES,)),
             pltpu.SemaphoreType.DMA((20,)),
-            pltpu.SemaphoreType.DMA((11,)),
+            pltpu.SemaphoreType.DMA((15,)),
         ],
         compiler_params=pltpu.CompilerParams(
             collective_id=0, has_side_effects=True, vmem_limit_bytes=63 * 2**20

time: 160 us -> 160 us (level)
  no operation moved by 1% of the time
where the time goes in v8:
time: 160 us
  Pallas kernels  159 us (99%)
    pallas_call x1, Pallas kernels, on_device(): pl.pallas_call(make_kernel(rows, feat, depth, hidden, micro, scale), out_...  156 us

profile of v8, /device:TPU:2, one launch (start us, length us, event | category | flops | bytes accessed | tf_op | source)
XLA Modules:
  0.0 159.8 jit_solution(17325993054283225700)
XLA Ops:
  0.6 156.4 %block_gradient.1 = (bf16[768,384]{1,0:T(8,128)(2,1)}, bf16[192,896]{1,0:T(8,128)(2,1)}, bf16[192,896]{1,0:T(8,128)(2,1)}) custom-call(bf16[768,384]{1,0:T(8,128)(2,1)} %tok_in.1, bf16[768,384]{1,0:T(8,128)(2,1)} %tgt_in.1, bf16[32,384]{1,0:T(8,128)(2,1)} %mod_in.1, f32[16,32]{1,0:T(8,128)} %bitcast.1, s32[3]{0:T(128)} %bins_in.1, s32[3]{0:T(128)} %grps_in.1, ...), custom_call_target="tpu_custom_call" | custom-call | flops 25367150592 | bytes 8388608 | tf_op jit(solution)/shard_map/block_gradient/pallas_call | solution.py:888
  157.0 2.6 %widen.1 = (f32[768,384]{1,0:T(8,128)}, f32[192,896]{1,0:T(8,128)}, f32[192,896]{1,0:T(8,128)}) custom-call(bf16[768,384]{1,0:T(8,128)(2,1)} %get-tuple-element.6.refs_0_, bf16[192,896]{1,0:T(8,128)(2,1)} %get-tuple-element.7.refs_1_, bf16[192,896]{1,0:T(8,128)(2,1)} %get-tuple-element.8.refs_2_), custom_call_target="tpu_custom_call" | custom-call | bytes 3833856 | tf_op jit(solution)/shard_map/widen/pallas_call | solution.py:863
